TPU v7x, 256 devices: a whole 4x4x8 slice. The times are simulated.
256 devices in a mesh: chan: 32 (over y, x, z_hi), tm: 8 (over z_lo, core).
Axes of the slice: x: 4, y: 4, z: 8 (z_hi: 2, z_lo: 4; z = z_hi * 4 + z_lo), core: 2. Of those that a mesh axis runs over, the one named last changes fastest.
Arguments:
- spectra: bfloat16 [1024, 128, 2, 1024], P('chan', 'tm'), may hold values from -6 to 6
- quality: int32 [1024, 128], P('chan', 'tm'), may hold values from 0 to 1, as said below
- plan: int32 [3], replicated, may hold values from 0 to 31, as said below
Outputs:
- correlations: float32 [96, 1024, 2048], P('tm', 'chan')
Inputs may be any that keep to these rules, and one draw needn't show every extreme that they name: `plan`: distinct channel block numbers; the first and the last block of the fibre are always among them. `quality`: 0 or 1; some channels are unusable in every segment.
All inputs are finite; a program needn't handle non-finite values.
Results may differ from a plain program's by a relative error of at most 0.0003.
Values may be sent and summed in bfloat16 or wider, within the bound.
A program may use at most 192 MiB of HBM per device.

v0:
```python
import math

import jax
import jax.numpy as jnp
from jax import lax
from jax.sharding import PartitionSpec as P

SRC_BLOCK = 32
SRC_BLOCKS = 3


def spread(value, axis, root):
    mine = lax.axis_index(axis) == root
    return lax.psum(jnp.where(mine, value, jnp.zeros_like(value)), axis)


def make_table(bins, lags):
    freq = lax.broadcasted_iota(jnp.int32, (bins, lags), 0)
    delay = lax.broadcasted_iota(jnp.int32, (bins, lags), 1) - bins
    phase = freq * delay % (2 * bins)
    angle = phase.astype(jnp.float32) * (math.pi / bins)
    scale = 1.0 / math.sqrt(bins)
    return jnp.concatenate([jnp.cos(angle) * scale, -jnp.sin(angle) * scale], axis=0)


def correlate(source, receiver):
    rotated = jnp.stack([receiver[:, :, 1], -receiver[:, :, 0]], axis=2)
    real_part = jnp.einsum("stpk,ctpk->sck", source, receiver, preferred_element_type=jnp.float32)
    imag_part = jnp.einsum("stpk,ctpk->sck", source, rotated, preferred_element_type=jnp.float32)
    return jnp.stack([real_part, imag_part], axis=2)


def shards(spectra, quality, plan):
    ch_dev = spectra.shape[0]
    bins = spectra.shape[3]
    owned = ch_dev // SRC_BLOCK
    local_mask = quality.astype(jnp.bfloat16)
    block_spec = []
    block_mask = []
    for which in range(SRC_BLOCKS):
        block = plan[which]
        owner = block // owned
        offset = block % owned * SRC_BLOCK
        piece = spectra
        flags = local_mask
        piece, flags = (spread(piece, "chan", owner), spread(flags, "chan", owner))
        block_spec.append(piece)
        block_mask.append(flags)
    source_spec = jnp.concatenate(block_spec, axis=0)
    source_mask = jnp.concatenate(block_mask, axis=0)
    masked_source = source_spec * source_mask[:, :, None, None]
    masked_local = spectra * local_mask[:, :, None, None]
    cross = correlate(masked_source, masked_local)
    counts = jnp.einsum("st,ct->sc", source_mask, local_mask, preferred_element_type=jnp.float32)
    share, pair_count = (
        lax.psum_scatter(cross, "tm", scatter_dimension=0, tiled=True),
        lax.psum_scatter(counts, "tm", scatter_dimension=0, tiled=True),
    )
    share_rows = share.shape[0]
    stacked = share / jnp.maximum(pair_count, 1.0)[:, :, None, None]
    table = make_table(bins, 2 * bins)
    flat = stacked.reshape(share_rows * ch_dev, 2 * bins)
    result = jnp.dot(
        flat, table, precision=lax.Precision.HIGHEST, preferred_element_type=jnp.float32
    )
    return result.reshape(share_rows, ch_dev, 2 * bins)


def solution(mesh):
    in_specs = (P("chan", "tm", None, None), P("chan", "tm"), P())
    out_specs = P("tm", "chan", None)
    return jax.shard_map(shards, mesh=mesh, in_specs=in_specs, out_specs=out_specs, check_vma=False)
```

profile of v0, /device:TPU:225, one launch (start us, length us, event | category | flops | bytes accessed | tf_op | source)
XLA Modules:
  0.0 1034.3 jit_solution(13398779334055474019)
XLA Ops:
  6.5 0.0 copy-start.2
  6.5 0.0 all-reduce.6.cloned.1.call-start
  6.5 1.4 fusion.12
  9.8 6.9 broadcast_select_fusion.2
  16.7 0.0 all-reduce.6.cloned.1.call-update
  16.8 0.0 reduce-scatter.4.cloned.1.call-start
  16.8 0.0 copy-done.2
  16.8 0.1 copy.18
  16.9 224.1 %all-reduce.2 = (bf16[32,16]{0,1:T(8,128)(2,1)S(1)}, bf16[32,16]{0,1:T(8,128)(2,1)S(1)}, bf16[32,16]{0,1:T(8,128)(2,1)S(1)}) all-reduce(bf16[32,16]{0,1:T(8,128)(2,1)S(1)} %get-tuple-element.21, bf16[32,16]{0,1:T(8,128)(2,1)S(1)} %get-tuple-element.20, ...), channel_id=1, replica_groups=mesh['chan'=32,'tm'=8] {'chan'}, use_global_device_ids=true, to_apply=%region_5.6 | all-reduce | flops 1536 | bytes 6144 | tf_op jit(solution)/shard_map/psum | solution.py:14
  241.1 0.1 pad_maximum_fusion.2
  241.1 0.1 copy.20
  241.2 2.0 copy_multiply_fusion
  243.2 12.8 %copy.21 = bf16[32,16,2,1024]{0,1,2,3:T(8,128)(2,1)} copy(bf16[32,16,2,1024]{3,1,2,0:T(8,128)(2,1)S(1)} %copy_multiply_fusion) | data formatting | bytes 4194304 | tf_op jit(solution)/shard_map/mul | solution.py:52
  256.1 0.1 fusion.11
  256.2 0.2 pad_maximum_fusion.1
  256.4 12.9 %copy.23 = bf16[32,16,2,1024]{0,1,2,3:T(8,128)(2,1)} copy(bf16[32,16,2,1024]{3,1,2,0:T(8,128)(2,1)S(1)} %pad_maximum_fusion.1) | data formatting | bytes 4194304 | tf_op jit(solution)/shard_map/stack | solution.py:27
  269.3 339.8 %all-reduce.6.cloned.1.call-done = (bf16[32,16,2,1024]{3,2,1,0:T(2,128)(2,1)}, bf16[32,16,2,1024]{3,2,1,0:T(2,128)(2,1)}, bf16[32,16,2,1024]{3,2,1,0:T(2,128)(2,1)}) async-done(((bf16[32,16,2,1024]{3,2,1,0:T(2,128)(2,1)}, bf16[32,16,2,1024]{3,2,1,0:T(2,128)(2,1)}, bf16[32,16,2,1024]{3,2,1,0:T(2,128)(2,1)}), (bf16[32,16,2,1024]{3,2,1,0:T(2,128)(2,1)}, bf16[32,16,2,1024]{3,2,1,0:T(2,128)(2,1)}, ...) | async-done | bytes 6291472 | tf_op jit(solution)/shard_map/psum | solution.py:14
  609.2 25.3 %maximum_multiply_fusion = bf16[96,16,2,1024]{3,2,1,0:T(2,128)(2,1)} fusion(bf16[32,16,2,1024]{3,2,1,0:T(2,128)(2,1)} %get-tuple-element.8, bf16[32,16,2,1024]{3,2,1,0:T(2,128)(2,1)} %get-tuple-element.9, bf16[32,16,2,1024]{3,2,1,0:T(2,128)(2,1)} %get-tuple-element.10, bf16[96,16]{1,0:T(8,128)(2,1)S(1)} %copy.20), kind=kLoop, calls=%fused_computation.18 | loop fusion | flops 9437184 | bytes 12585984 | tf_op jit(solution)/shard_map/mul | solution.py:51
  634.4 15.7 %copy.22 = bf16[96,16,2,1024]{0,1,2,3:T(8,128)(2,1)} copy(bf16[96,16,2,1024]{3,2,1,0:T(2,128)(2,1)} %maximum_multiply_fusion) | data formatting | bytes 12582912 | tf_op jit(solution)/shard_map/mul | solution.py:51
  650.2 0.0 copy-start
  650.2 12.7 %convolution_bitcast_fusion.1 = f32[96,32,1,1024]{0,1,3,2:T(8,128)} fusion(bf16[32,16,2,1024]{0,1,2,3:T(8,128)(2,1)} %copy.21, bf16[96,16,2,1024]{0,1,2,3:T(8,128)(2,1)} %copy.22), kind=kOutput, calls=%fused_computation.9 | convolution fusion | flops 201326592 | bytes 20971520 | tf_op jit(solution)/shard_map/stpk,ctpk->sck/dot_general | solution.py:28
  662.8 0.0 copy-done
  662.8 9.4 convolution_bitcast_fusion
  672.3 23.4 %pad_maximum_fusion = f32[96,32,2,1024]{0,1,3,2:T(8,128)} fusion(f32[96,32,1,1024]{0,1,3,2:T(8,128)} %convolution_bitcast_fusion, f32[96,32,1,1024]{0,1,3,2:T(8,128)} %convolution_bitcast_fusion.1), kind=kLoop, calls=%fused_computation | loop fusion | flops 6291456 | bytes 50331648 | tf_op jit(solution)/shard_map/stack | solution.py:30
  695.7 32.0 %copy.25 = f32[96,32,2,1024]{3,1,2,0:T(8,128)} copy(f32[96,32,2,1024]{0,1,3,2:T(8,128)} %pad_maximum_fusion) | data formatting | bytes 50331648 | tf_op jit(solution)/shard_map/stack | solution.py:30
  727.7 0.0 reduce-scatter.4.cloned.1.call-update
  727.7 0.2 fusion.13
  727.9 31.6 %fusion = f32[16,32]{1,0:T(8,128)S(1)} fusion(f32[96,32]{1,0:T(8,128)S(1)} %fusion.13), kind=kCustom, calls=%all-reduce-scatter | all-reduce-scatter fusion | flops 4097 | bytes 15360
  759.5 1.3 collective-permute-start
  760.8 1.5 collective-permute-start.1
  762.3 0.0 copy-start.3
  762.3 34.9 %cosine_multiply_fusion = (f32[1024,2048]{1,0:T(8,128)}, f32[1024,2048]{1,0:T(8,128)}) fusion(s32[2048]{0:T(1024)S(1)} %iota_add_fusion), kind=kLoop, calls=%fused_computation.14 | loop fusion | flops 35651584 | bytes 16785408 | tf_op jit(solution)/shard_map/mul | solution.py:23
  797.2 0.0 copy-done.3
  797.2 0.6 dynamic-slice.4
  798.5 0.0 collective-permute-done.1
  798.5 0.0 collective-permute-done
  798.5 0.2 concatenate.12
  798.8 200.8 %reduce-scatter.4.cloned.1.call-done = f32[12,32,2,1024]{3,1,2,0:T(8,128)} async-done(((f32[96,32,2,1024]{3,1,2,0:T(8,128)}), f32[12,32,2,1024]{3,1,2,0:T(8,128)}) %reduce-scatter.4.cloned.1.call-update) | async-done | bytes 3145744 | tf_op jit(solution)/shard_map/reduce_scatter | solution.py:56
  999.6 0.0 copy-start.1
  999.6 2.4 divide_bitcast_fusion
  1002.0 0.4 copy.29
  1002.4 1.5 copy-done.1
  1003.9 23.6 %fusion.1 = f32[12,32,2048]{2,1,0:T(8,128)} fusion(f32[12,32,2048]{2,1,0:T(8,128)S(1)} %bitcast.33, f32[1024,2048]{1,0:T(8,128)} %get-tuple-element.19, f32[1024,2048]{1,0:T(8,128)S(1)} %copy-done.1), kind=kOutput, calls=%fused_computation.2 | convolution fusion | flops 19331547136 | bytes 23068672 | tf_op jit(solution)/shard_map/dot_general | solution.py:63
  (5 shorter events, 0.0 us)
Async XLA Ops:
  6.5 10.3 copy-start.2
  6.5 602.6 %all-reduce.6.cloned.1.call-start = ((), (), s32[]{:S(2)}) async-start(), calls=%async_computation.2 | async-start | bytes 12582912 | tf_op jit(solution)/shard_map/psum | solution.py:14
  16.8 982.8 %reduce-scatter.4.cloned.1.call-start = ((), (), s32[]{:S(2)}) async-start(), calls=%async_computation.1 | async-start | bytes 28311552 | tf_op jit(solution)/shard_map/reduce_scatter | solution.py:56
  650.2 12.7 %copy-start = (bf16[96,16,2,1024]{0,1,2,3:T(8,128)(2,1)S(1)}, bf16[96,16,2,1024]{0,1,2,3:T(8,128)(2,1)}, u32[]{:S(2)}) copy-start(bf16[96,16,2,1024]{0,1,2,3:T(8,128)(2,1)} %copy.22) | copy-start | bytes 18874372
  759.5 39.0 %collective-permute-start = (f32[16,32]{1,0:T(8,128)S(1)}, f32[16,32]{1,0:T(8,128)S(1)}, u32[]{:S(2)}, u32[]{:S(2)}) collective-permute-start(f32[16,32]{1,0:T(8,128)S(1)} %fusion), channel_id=1, source_target_pairs={{0,1},{1,2},{2,3},{3,4},{4,5},{5,6},{6,7},{8,9},{9,10},{10,11},{11... | collective-permute-start | bytes 6152
  760.8 37.7 %collective-permute-start.1 = (f32[12,32]{1,0:T(8,128)S(1)}, f32[12,32]{1,0:T(8,128)S(1)}, u32[]{:S(2)}, u32[]{:S(2)}) collective-permute-start(f32[12,32]{1,0:T(8,128)S(1)} %slice.22), channel_id=1, source_target_pairs={{0,2},{1,3},{2,4},{3,5},{4,6},{5,7},{8,10},{9,11},{10,12},{11,13},... | collective-permute-start | bytes 4616
  762.3 34.9 %copy-start.3 = (u32[256]{0:T(256)S(1)}, u32[256]{0:T(256)}, u32[]{:S(2)}) copy-start(u32[256]{0:T(256)} %constant.60) | copy-start | bytes 3076
  999.6 4.3 copy-start.1
Sparse Core Ops, SparseCore 0:
  16.9 592.2 all-reduce.5
  727.8 271.7 reduce-scatter.3
where the time goes:
time: 1040 us; the launch traced here: 1030 us
  waiting for transfers between devices  541 us (52%)
  blocking collectives  256 us (25%)
  other arithmetic  95.4 us (9%)
  local copies, waits for them, and re-layouts  77.8 us (7%)
  matrix products  45.9 us (4%)
  between operations  16.1 us (2%)
    psum x1, waiting for transfers between devices, spread(): return lax.psum(jnp.where(mine, value, jnp.zeros_like(value)), axis)  340 us
    psum x1, blocking collectives, spread(): return lax.psum(jnp.where(mine, value, jnp.zeros_like(value)), axis)  224 us
    reduce_scatter x1, waiting for transfers between devices, shards(): lax.psum_scatter(cross, 'tm', scatter_dimension=0, tiled=True)  201 us
    mul x1, other arithmetic, make_table(): jnp.cos(angle) * scale  34.9 us
    another operation x1, local copies, waits for them, and re-layouts, correlate(): return jnp.stack([real_part, imag_part], axis=2)  32 us
    unnamed x1, blocking collectives  31.6 us
    mul x1, other arithmetic, shards(): masked_source = source_spec * source_mask[:, :, None, None]  25.3 us
    dot_general x1, matrix products, shards(): jnp.dot(flat, table, precision=lax.Precision.HIGHEST, preferred_element_t...  23.6 us
  transfers between devices with their start and end apart: 4, of which 2 were waited for; matrix products, arithmetic and copies ran while one was open for 9% of the time, Pallas kernels for 0%

commit v1 on v0

v1 whole, which is shorter than its diff:
```python
import functools
import math

import jax
import jax.numpy as jnp
from jax import lax
from jax.experimental import pallas as pl
from jax.experimental.pallas import tpu as pltpu
from jax.sharding import PartitionSpec as P

MESH = pl.DeviceIdType.MESH
ANY = pl.ANY
SRC = 3
NX = NY = 4
NTM = 8
CH = 32
SEG = 16
BINS = 1024
KB = BINS // NTM
ROWS = SRC * KB + CH
BIG = 56 * 1024 * 1024


def place():
    ch = lax.axis_index("chan")
    return ch // 8, lax.rem(ch // 2, 4), lax.rem(ch, 2), lax.axis_index("tm")


def device(y, x, zh, tm):
    return ((y * 4 + x) * 2 + zh, tm)


def up(v, d):
    return lax.rem(v + d, 4)


def greet(devices):
    bar = pltpu.get_barrier_semaphore()
    for d in devices:
        pl.semaphore_signal(bar, inc=1, device_id=d, device_id_type=MESH)
    pl.semaphore_wait(bar, len(devices))


def remote(src, dst, send, recv, where):
    copy = pltpu.make_async_remote_copy(
        src_ref=src, dst_ref=dst, send_sem=send, recv_sem=recv, device_id=where, device_id_type=MESH
    )
    copy.start()
    return copy


def exchange_body(plan, m, y_out, rx, sx, ry, sy, rz, sh, send, recv, local):
    y, x, zh, tm = place()
    tms = [lax.rem(tm + d, NTM) for d in range(1, NTM)]
    greet(
        [device(y, x, zh, t) for t in tms]
        + [device(y, up(x, d), zh, tm) for d in (1, 2, 3)]
        + [device(up(y, d), x, zh, tm) for d in (1, 2, 3)]
        + [device(y, x, 1 - zh, tm)]
    )
    ox = [lax.rem(plan[b] // 2, 4) for b in range(SRC)]
    oy = [plan[b] // 8 for b in range(SRC)]
    oz = [lax.rem(plan[b], 2) for b in range(SRC)]

    stage_x = []
    for d in (1, 3, 2):
        to = up(x, d)
        stage_x.append(
            remote(m.at[pl.ds(to * 8, 8)], rx.at[x], send.at[d], recv.at[d], device(y, to, zh, tm))
        )
    own_x = pltpu.make_async_copy(m.at[pl.ds(x * 8, 8)], rx.at[x], local.at[0])
    own_x.start()
    main = []
    for d in range(1, NTM):
        t = tms[d - 1]
        lanes = pl.ds(pl.multiple_of(t * KB, KB), KB)
        rows = pl.ds(pl.multiple_of(tm * SEG, SEG), SEG)
        main.append(
            remote(
                m.at[:, :, :, lanes],
                y_out.at[pl.ds(0, CH + 1), :, rows, :],
                send.at[8 + d],
                recv.at[8 + d],
                device(y, x, zh, t),
            )
        )
    my_lanes = pl.ds(pl.multiple_of(tm * KB, KB), KB)
    my_rows = pl.ds(pl.multiple_of(tm * SEG, SEG), SEG)
    own_m = pltpu.make_async_copy(
        m.at[:, :, :, my_lanes], y_out.at[pl.ds(0, CH + 1), :, my_rows, :], local.at[1]
    )
    own_m.start()

    own_x.wait()
    for c in stage_x:
        c.wait_recv()
    for b in range(SRC):

        def pick_x(i, carry, b=b):
            sx[b, i] = rx[ox[b], i]
            return carry

        lax.fori_loop(0, 8, pick_x, 0)
    stage_y = []
    for d in (1, 3, 2):
        to = up(y, d)
        stage_y.append(
            remote(
                sx.at[:, pl.ds(to * 2, 2)],
                ry.at[y],
                send.at[4 + d],
                recv.at[4 + d],
                device(to, x, zh, tm),
            )
        )
    own_y = pltpu.make_async_copy(sx.at[:, pl.ds(y * 2, 2)], ry.at[y], local.at[2])
    own_y.start()
    own_y.wait()
    for c in stage_y:
        c.wait_recv()
    for b in range(SRC):

        def pick_y(i, carry, b=b):
            sy[i, b] = ry[oy[b], b, i]
            return carry

        lax.fori_loop(0, 2, pick_y, 0)
    stage_z = remote(sy.at[1 - zh], rz.at[zh], send.at[0], recv.at[0], device(y, x, 1 - zh, tm))
    own_z = pltpu.make_async_copy(sy.at[zh], rz.at[zh], local.at[3])
    own_z.start()
    own_z.wait()
    stage_z.wait_recv()
    for b in range(SRC):
        sh[b] = rz[oz[b], b]
    shares = []
    for d in range(1, NTM):
        t = tms[d - 1]
        lanes = pl.ds(pl.multiple_of(t * KB, KB), KB)
        shares.append(
            remote(
                sh.at[:, :, :, lanes],
                y_out.at[pl.ds(CH + 1, SRC), :, my_rows, :],
                send.at[16 + d],
                recv.at[16 + d],
                device(y, x, zh, t),
            )
        )
    own_s = pltpu.make_async_copy(
        sh.at[:, :, :, my_lanes], y_out.at[pl.ds(CH + 1, SRC), :, my_rows, :], local.at[4]
    )
    own_s.start()
    own_s.wait()
    own_m.wait()
    for c in stage_x + stage_y + [stage_z]:
        c.wait_send()
    for c in main + shares:
        c.wait()


def exchange(plan, m):
    bf = jnp.bfloat16
    return pl.pallas_call(
        exchange_body,
        out_shape=jax.ShapeDtypeStruct((CH + 1 + SRC, 2, NTM * SEG, KB), bf),
        in_specs=[pl.BlockSpec(memory_space=pltpu.SMEM), pl.BlockSpec(memory_space=ANY)],
        out_specs=pl.BlockSpec(memory_space=ANY),
        scratch_shapes=[
            pltpu.VMEM((4, 8, 2, SEG, BINS), bf),
            pltpu.VMEM((SRC, 8, 2, SEG, BINS), bf),
            pltpu.VMEM((4, SRC, 2, 2, SEG, BINS), bf),
            pltpu.VMEM((2, SRC, 2, SEG, BINS), bf),
            pltpu.VMEM((2, SRC, 2, SEG, BINS), bf),
            pltpu.VMEM((SRC, 2, SEG, BINS), bf),
            pltpu.SemaphoreType.DMA((24,)),
            pltpu.SemaphoreType.DMA((24,)),
            pltpu.SemaphoreType.DMA((5,)),
        ],
        compiler_params=pltpu.CompilerParams(
            collective_id=0, has_side_effects=True, vmem_limit_bytes=BIG
        ),
    )(plan, m)


def share_body(y_ref, s_ref):
    for b in range(SRC):
        for p in range(2):
            s_ref[pl.ds(b * KB, KB), pl.ds(p * 128, 128)] = (
                y_ref[1 + b, p].astype(jnp.float32).T.astype(jnp.bfloat16)
            )
    for p in range(2):
        flags = y_ref[0, p].astype(jnp.float32).T[:CH]
        s_ref[pl.ds(SRC * KB, CH), pl.ds(p * 128, 128)] = flags.astype(jnp.bfloat16)


def share(y):
    return pl.pallas_call(
        share_body,
        grid=(1,),
        out_shape=jax.ShapeDtypeStruct((ROWS, 256), jnp.bfloat16),
        in_specs=[pl.BlockSpec((4, 2, 128, KB), lambda g: (8, 0, 0, 0))],
        out_specs=pl.BlockSpec((ROWS, 256), lambda g: (0, 0)),
    )(y)


def gather_body(s_ref, o_ref, send, recv, local):
    y, x, zh, tm = place()
    near = [
        device(y, up(x, 1), zh, tm),
        device(y, up(x, 3), zh, tm),
        device(up(y, 1), x, zh, tm),
        device(up(y, 3), x, zh, tm),
        device(y, x, 1 - zh, tm),
    ]
    greet(near)
    cut = ROWS // 32 * 16
    me = y * 4 + x
    own = pltpu.make_async_copy(s_ref, o_ref.at[zh, me], local)
    own.start()
    across = remote(s_ref, o_ref.at[zh, me], send.at[0], recv.at[0], near[4])
    started = []
    full, low, high = pl.ds(0, ROWS), pl.ds(0, cut), pl.ds(cut, ROWS - cut)

    def put(half, slot, part, k, where):
        ref = o_ref.at[half, slot, part]
        copy = remote(ref, ref, send.at[k], recv.at[k], where)
        started.append(copy)
        return copy

    class Half:
        def __init__(self, half):
            self.half = half
            first, second = (near[:2], near[2:4]) if half == 0 else (near[2:4], near[:2])
            self.ap, self.am = first
            self.bp, self.bm = second
            self.a, self.b = (x, y) if half == 0 else (y, x)
            self.base = 1 + 20 * half
            self.sent = {}
            self.passed = {}

        def slot(self, b, a):
            return b * 4 + a if self.half == 0 else a * 4 + b

        def at(self, r):
            return up(self.a, (0, 3, 1, 2)[r])

        def send_b(self, r):
            k = self.base + 4 + 4 * r
            slot = self.slot(self.b, self.at(r))
            self.sent[r] = (
                put(self.half, slot, full, k, self.bp),
                put(self.half, slot, full, k + 1, self.bm),
            )

        def start(self):
            slot = self.slot(self.b, self.a)
            self.a1 = put(self.half, slot, full, self.base, self.ap)
            self.a2 = put(self.half, slot, full, self.base + 1, self.am)
            self.send_b(0)

        def first(self):
            self.a1.wait_recv()
            self.a3 = put(self.half, self.slot(self.b, self.at(1)), low, self.base + 2, self.ap)
            self.send_b(1)
            self.a2.wait_recv()
            self.a4 = put(self.half, self.slot(self.b, self.at(2)), high, self.base + 3, self.am)
            self.send_b(2)

        def second(self):
            self.a3.wait_recv()
            self.a4.wait_recv()
            self.send_b(3)

        def forward(self, r):
            k = self.base + 4 + 4 * r
            a = self.at(r)
            plus, minus = self.sent[r]
            plus.wait_recv()
            f1 = put(self.half, self.slot(up(self.b, 3), a), low, k + 2, self.bp)
            minus.wait_recv()
            f2 = put(self.half, self.slot(up(self.b, 1), a), high, k + 3, self.bm)
            self.passed[r] = (f1, f2)

    own.wait()
    across.wait_recv()
    halves = [Half(0), Half(1)]
    for h in halves:
        h.start()
    for h in halves:
        h.first()
    for h in halves:
        h.forward(0)
    for h in halves:
        h.second()
    for r in (1, 2, 3):
        for h in halves:
            h.forward(r)
    for r in range(4):
        for h in halves:
            for f in h.passed[r]:
                f.wait_recv()
    across.wait_send()
    for copy in started:
        copy.wait_send()


def gather(s):
    return pl.pallas_call(
        gather_body,
        out_shape=jax.ShapeDtypeStruct((2, 16, ROWS, 256), jnp.bfloat16),
        in_specs=[pl.BlockSpec(memory_space=ANY)],
        out_specs=pl.BlockSpec(memory_space=ANY),
        scratch_shapes=[
            pltpu.SemaphoreType.DMA((41,)),
            pltpu.SemaphoreType.DMA((41,)),
            pltpu.SemaphoreType.DMA,
        ],
        compiler_params=pltpu.CompilerParams(collective_id=1, has_side_effects=True),
    )(s)


def correlate_body(plan, g_ref, y_ref, out_ref, sa, sq, ra, rq, ob):
    f32, bf = jnp.float32, jnp.bfloat16

    def widen(j, carry):
        zh, y, x = lax.rem(j, 2), lax.rem(j // 2, 4), j // 8
        for b in range(SRC):
            rows = pl.ds(pl.multiple_of((b * CH + j) * KB, KB), KB)
            for p, part in enumerate((sa, sq)):
                lanes = pl.ds(p * 128, 128)
                part[rows, :] = g_ref[zh, y * 4 + x, pl.ds(b * KB, KB), lanes].astype(f32)
        rows = pl.ds(pl.multiple_of(j * KB, KB), KB)
        for p, part in enumerate((ra, rq)):
            part[rows, :] = y_ref[j, p].astype(f32).T
        return carry

    lax.fori_loop(0, CH, widen, 0)
    fr = y_ref[CH, 0].astype(f32).T[:CH]
    fr = jnp.concatenate([fr, fr], axis=0).astype(bf)
    counts = []
    for b in range(SRC):
        fs = g_ref[lax.rem(plan[b], 2), plan[b] // 2, pl.ds(SRC * KB, CH), pl.ds(0, 128)]
        counts.append(
            lax.dot_general(fs, fr, (((1,), (1,)), ((), ())), preferred_element_type=f32)
        )
    inverse = 1.0 / jnp.maximum(jnp.concatenate(counts, axis=0), 1.0)

    def one(k):
        sources, channels = pl.ds(k, SRC * CH, stride=KB), pl.ds(k, CH, stride=KB)
        s = jnp.concatenate([sa[sources, :], sq[sources, :]], axis=1).astype(bf)
        a, q = ra[channels, :], rq[channels, :]
        real, imag = jnp.concatenate([a, q], axis=1), jnp.concatenate([q, -a], axis=1)
        both = jnp.concatenate([real, imag], axis=0).astype(bf)
        res = lax.dot_general(s, both, (((1,), (1,)), ((), ())), preferred_element_type=f32)
        res = res * inverse
        ob[sources, :] = jnp.concatenate([res, jnp.zeros_like(res)], axis=1)

    def some(i, carry):
        for u in range(8):
            one(i * 8 + u)
        return carry

    lax.fori_loop(0, KB // 8, some, 0)

    def turn(i, carry):
        for u in range(4):
            s = i * 4 + u
            out_ref[s] = ob[pl.ds(pl.multiple_of(s * KB, KB), KB), pl.ds(0, 2 * CH)].T
        return carry

    lax.fori_loop(0, SRC * CH // 4, turn, 0)


def correlate(plan, g, y):
    vmem = pl.BlockSpec(memory_space=pltpu.VMEM)
    return pl.pallas_call(
        correlate_body,
        out_shape=jax.ShapeDtypeStruct((SRC * CH, 2 * CH, KB), jnp.float32),
        in_specs=[pl.BlockSpec(memory_space=pltpu.SMEM), vmem, vmem],
        out_specs=vmem,
        scratch_shapes=[
            pltpu.VMEM((SRC * CH * KB, 128), jnp.float32),
            pltpu.VMEM((SRC * CH * KB, 128), jnp.float32),
            pltpu.VMEM((CH * KB, 128), jnp.float32),
            pltpu.VMEM((CH * KB, 128), jnp.float32),
            pltpu.VMEM((SRC * CH * KB, 128), jnp.float32),
        ],
        compiler_params=pltpu.CompilerParams(vmem_limit_bytes=BIG),
    )(plan, g, y)


def collect_body(x_ref, v_ref, send, recv, local):
    y, x, zh, tm = place()
    tms = [lax.rem(tm + d, NTM) for d in range(1, NTM)]
    greet([device(y, x, zh, t) for t in tms])
    copies = []
    for d in range(1, NTM):
        t = tms[d - 1]
        copies.append(
            remote(x_ref.at[t], v_ref.at[tm], send.at[d], recv.at[d], device(y, x, zh, t))
        )
    own = pltpu.make_async_copy(x_ref.at[tm], v_ref.at[tm], local)
    own.start()
    own.wait()
    for c in copies:
        c.wait()


def collect(x):
    return pl.pallas_call(
        collect_body,
        out_shape=jax.ShapeDtypeStruct(x.shape, x.dtype),
        in_specs=[pl.BlockSpec(memory_space=ANY)],
        out_specs=pl.BlockSpec(memory_space=ANY),
        scratch_shapes=[
            pltpu.SemaphoreType.DMA((NTM,)),
            pltpu.SemaphoreType.DMA((NTM,)),
            pltpu.SemaphoreType.DMA,
        ],
        compiler_params=pltpu.CompilerParams(collective_id=2, has_side_effects=True),
    )(x)


def make_table():
    tau = lax.broadcasted_iota(jnp.int32, (1, 2 * BINS), 1) - BINS

    def pair(count, step):
        freq = lax.broadcasted_iota(jnp.int32, (count, 1), 0) * step
        angle = ((freq * tau) % (2 * BINS)).astype(jnp.float32) * (math.pi / BINS)
        return jnp.cos(angle), jnp.sin(angle)

    c1, s1 = (v[:, None, :] for v in pair(BINS // 8, 8))
    c2, s2 = (v[None, :, :] / math.sqrt(BINS) for v in pair(8, 1))
    shape = (BINS, 2 * BINS)
    table = jnp.concatenate(
        [(c1 * c2 - s1 * s2).reshape(shape), -(s1 * c2 + c1 * s2).reshape(shape)], axis=0
    )
    high = lax.reduce_precision(table, 8, 7)
    return high.astype(jnp.bfloat16), (table - high).astype(jnp.bfloat16)


def lags_body(v_ref, th_ref, tl_ref, out_ref, xh, xl):
    @pl.when(pl.program_id(0) == 0)
    def _():
        def split(s, carry):
            rows = pl.ds(pl.multiple_of(s * CH, CH), CH)
            for p in range(2):
                for j in range(NTM):
                    lanes = pl.ds(p * BINS + j * KB, KB)
                    value = v_ref[j, s, p]
                    high = value.astype(jnp.bfloat16)
                    xh[rows, lanes] = high
                    xl[rows, lanes] = (value - high.astype(jnp.float32)).astype(jnp.bfloat16)
            return carry

        lax.fori_loop(0, 12, split, 0)

    def dot(a, b):
        return jnp.dot(a, b, preferred_element_type=jnp.float32)

    th = th_ref[...]
    h = xh[...]
    out_ref[...] = dot(xl[...], th) + dot(h, tl_ref[...]) + dot(h, th)


def lags(v, th, tl):
    rows, wide, step = 12 * CH, 2 * BINS, 256
    return pl.pallas_call(
        lags_body,
        grid=(wide // step,),
        out_shape=jax.ShapeDtypeStruct((rows, wide), jnp.float32),
        in_specs=[
            pl.BlockSpec((NTM, 12, 2, CH, KB), lambda g: (0, 0, 0, 0, 0)),
            pl.BlockSpec((wide, step), lambda g: (0, g)),
            pl.BlockSpec((wide, step), lambda g: (0, g)),
        ],
        out_specs=pl.BlockSpec((rows, step), lambda g: (0, g)),
        scratch_shapes=[
            pltpu.VMEM((rows, wide), jnp.bfloat16),
            pltpu.VMEM((rows, wide), jnp.bfloat16),
        ],
        compiler_params=pltpu.CompilerParams(vmem_limit_bytes=BIG),
    )(v, th, tl)


def shards(spectra, quality, plan):
    flags = quality.astype(jnp.bfloat16)
    masked = (spectra * flags[:, :, None, None]).transpose(0, 2, 1, 3)
    row = jnp.tile(jnp.pad(flags.T, ((0, 0), (0, KB - CH))), (1, NTM))
    m = jnp.concatenate([masked, jnp.broadcast_to(row, (1, 2, SEG, BINS))], axis=0)
    th, tl = make_table()
    y = exchange(plan, m)
    g = gather(share(y))
    x = correlate(plan, g, y)
    v = collect(x.reshape(NTM, 12 * 2 * CH, KB))
    out = lags(v.reshape(NTM, 12, 2, CH, KB), th, tl)
    return out.reshape(12, CH, 2 * BINS)


def solution(mesh):
    in_specs = (P("chan", "tm", None, None), P("chan", "tm"), P())
    out_specs = P("tm", "chan", None)
    return jax.shard_map(shards, mesh=mesh, in_specs=in_specs, out_specs=out_specs, check_vma=False)
```

time: 1040 us -> 258 us (0.25)
  waiting for transfers between devices: 541 us -> 0 us
  blocking collectives: 256 us -> 0 us
  Pallas kernels: 0 us -> 238 us
  other arithmetic: 95.4 us -> 15.9 us
  local copies, waits for them, and re-layouts: 77.8 us -> 0.13 us
  matrix products: 45.9 us -> 0 us
  between operations: 16.1 us -> 0.11 us
    psum x1 -> x0, waiting for transfers between devices: 340 us -> none  [spread(): return lax.psum(jnp.where(mine, value, jnp.zeros_like(value)), axis)]
    pallas_call x0 -> x6, Pallas kernels: none -> 238 us  [the longest x1 78.4 us: collect(): pl.pallas_call(collect_body, out_shape=jax.ShapeDtypeStruct(x.shape, x.dt...]
    psum x1 -> x0, blocking collectives: 224 us -> none  [spread(): return lax.psum(jnp.where(mine, value, jnp.zeros_like(value)), axis)]
    reduce_scatter x1 -> x0, waiting for transfers between devices: 201 us -> none  [shards(): lax.psum_scatter(cross, 'tm', scatter_dimension=0, tiled=True)]
    mul x3 -> x1, other arithmetic: 62.2 us -> 0.01 us  [pair(): freq = lax.broadcasted_iota(jnp.int32, (count, 1), 0) * step]
    dot_general x4 -> x0, matrix products: 45.9 us -> none  [the longest x1 23.6 us: shards(): jnp.dot(flat, table, precision=lax.Precision.HIGHEST, preferred_element_t...]
    another operation x2 -> x1, local copies, waits for them, and re-layouts: 44.9 us -> 0.01 us  [shards(): row = jnp.tile(jnp.pad(flags.T, ((0, 0), (0, KB - CH))), (1, NTM))]
    unnamed x1 -> x0, blocking collectives: 31.6 us -> none
  transfers between devices with their start and end apart: 4 -> 0, of which waited for: 2 -> 0; matrix products, arithmetic and copies ran while one was open for 9% -> 0% of each run, Pallas kernels for 0% -> 0%
where the time goes in v1:
time: 258 us; the launch traced here: 254 us
  Pallas kernels  238 us (92%)
  other arithmetic  15.9 us (6%)
    pallas_call x1, Pallas kernels, collect(): pl.pallas_call(collect_body, out_shape=jax.ShapeDtypeStruct(x.shape, x.dt...  78.4 us
    pallas_call x1, Pallas kernels, exchange(): pl.pallas_call(exchange_body, out_shape=jax.ShapeDtypeStruct((CH + 1 + SR...  67.4 us
    pallas_call x1, Pallas kernels, gather(): pl.pallas_call(gather_body, out_shape=jax.ShapeDtypeStruct((2, 16, ROWS,...  49 us
    pallas_call x1, Pallas kernels, correlate(): pl.pallas_call(correlate_body, out_shape=jax.ShapeDtypeStruct((SRC * CH,...  24.9 us
    pallas_call x1, Pallas kernels, lags(): pl.pallas_call(lags_body, grid=(wide // step,), out_shape=jax.ShapeDtypeS...  16.5 us
    convert_element_type x1, other arithmetic, make_table(): return (high.astype(jnp.bfloat16), (table - high).astype(jnp.bfloat16))  7.09 us

profile of v1, /device:TPU:225, one launch (start us, length us, event | category | flops | bytes accessed | tf_op | source)
XLA Modules:
  0.0 254.0 jit_solution(8381447985590649513)
XLA Ops:
  0.0 4.1 %fusion.6 = (f32[128,2048]{1,0:T(8,128)S(1)}, f32[128,2048]{1,0:T(8,128)S(1)}) fusion(s32[2048]{0:T(1024)S(1)} %iota_add_fusion, s32[128]{0:T(128)S(1)} %iota_multiply_fusion), kind=kLoop, calls=%fused_computation.18 | loop fusion | flops 3670016 | bytes 2105856 | tf_op jit(solution)/shard_map/cos | solution.py:429
  4.1 0.3 cosine_multiply_fusion
  4.4 2.5 subtract_bitcast_fusion
  6.9 0.0 copy-start.1
  6.9 0.0 copy-start
  6.9 7.1 %fusion = (bf16[2048,2048]{1,0:T(8,128)(2,1)}, bf16[2048,2048]{1,0:T(8,128)(2,1)}) fusion(f32[1024,2048]{1,0:T(8,128)S(1)} %get-tuple-element.8, f32[1024,2048]{1,0:T(8,128)S(1)} %get-tuple-element.7), kind=kLoop, calls=%fused_computation.2 | loop fusion | flops 20971520 | bytes 33554432 | tf_op jit(solution)/shard_map/convert_element_type | solution.py:438
  14.0 0.0 copy-done.1
  14.0 0.1 copy.4
  14.1 0.0 copy-done
  14.1 0.4 fusion.1
  14.6 1.5 pad_maximum_fusion.1.m
  16.1 67.4 %shard_map.37.y_ref = bf16[36,2,128,128]{3,2,1,0:T(8,128)(2,1)} custom-call(s32[3]{0:T(128)} %plan.3, bf16[33,2,16,1024]{3,2,1,0:T(8,128)(2,1)} %pad_maximum_fusion.1.m), custom_call_target="tpu_custom_call" | custom-call | tf_op jit(solution)/shard_map/pallas_call | solution.py:162
  83.5 1.8 shard_map.38.s_ref
  85.3 49.0 %shard_map.39.g_ref = bf16[2,16,416,256]{3,2,1,0:T(8,128)(2,1)} custom-call(bf16[416,256]{1,0:T(8,128)(2,1)} %shard_map.38.s_ref), custom_call_target="tpu_custom_call" | custom-call | tf_op jit(solution)/shard_map/pallas_call | solution.py:307
  134.3 24.9 %shard_map.40 = f32[96,64,128]{2,1,0:T(8,128)} custom-call(s32[3]{0:T(128)} %plan.3, bf16[2,16,416,256]{3,2,1,0:T(8,128)(2,1)} %shard_map.39.g_ref, bf16[36,2,128,128]{3,2,1,0:T(8,128)(2,1)} %shard_map.37.y_ref), custom_call_target="tpu_custom_call" | custom-call | tf_op jit(solution)/shard_map/pallas_call | solution.py:375
  159.2 78.4 %shard_map.41 = f32[8,768,128]{2,1,0:T(8,128)} custom-call(f32[8,768,128]{2,1,0:T(8,128)} %bitcast.15), custom_call_target="tpu_custom_call" | custom-call | tf_op jit(solution)/shard_map/pallas_call | solution.py:409
  237.6 16.5 %shard_map.42 = f32[384,2048]{1,0:T(8,128)} custom-call(f32[8,12,2,32,128]{4,3,2,1,0:T(8,128)} %bitcast.16, bf16[2048,2048]{1,0:T(8,128)(2,1)} %get-tuple-element.6.th_ref, bf16[2048,2048]{1,0:T(8,128)(2,1)} %get-tuple-element.5.tl_ref), custom_call_target="tpu_custom_call" | custom-call | tf_op jit(solution)/shard_map/pallas_call | solution.py:467
  (8 shorter events, 0.0 us)
Async XLA Ops:
  6.9 7.1 %copy-start.1 = (s32[32,16]{0,1:T(8,128)S(1)}, s32[32,16]{0,1:T(8,128)}, u32[]{:S(2)}) copy-start(s32[32,16]{0,1:T(8,128)} %param.4) | copy-start | bytes 6148
  6.9 7.2 %copy-start = (bf16[32,16,2,1024]{3,2,1,0:T(2,128)(2,1)S(1)}, bf16[32,16,2,1024]{3,2,1,0:T(2,128)(2,1)}, u32[]{:S(2)}) copy-start(bf16[32,16,2,1024]{3,2,1,0:T(2,128)(2,1)} %param.3) | copy-start | bytes 6291460

commit v2 on v1

v2 whole, which is shorter than its diff:
```python
import functools
import math

import jax
import jax.numpy as jnp
from jax import lax
from jax.experimental import pallas as pl
from jax.experimental.pallas import tpu as pltpu
from jax.sharding import PartitionSpec as P

MESH = pl.DeviceIdType.MESH
ANY = pl.ANY
SRC = 3
NX = NY = 4
NTM = 8
CH = 32
SEG = 16
BINS = 1024
KB = BINS // NTM
ROWS = SRC * KB + CH
EARLY = 16
TOP = 32766.0
BIG = 56 * 1024 * 1024


def place():
    ch = lax.axis_index("chan")
    return ch // 8, lax.rem(ch // 2, 4), lax.rem(ch, 2), lax.axis_index("tm")


def device(y, x, zh, tm):
    return ((y * 4 + x) * 2 + zh, tm)


def up(v, d):
    return lax.rem(v + d, 4)


def greet(devices):
    bar = pltpu.get_barrier_semaphore()
    for d in devices:
        pl.semaphore_signal(bar, inc=1, device_id=d, device_id_type=MESH)
    pl.semaphore_wait(bar, len(devices))


def remote(src, dst, send, recv, where):
    copy = pltpu.make_async_remote_copy(
        src_ref=src, dst_ref=dst, send_sem=send, recv_sem=recv, device_id=where, device_id_type=MESH
    )
    copy.start()
    return copy


def front_body(plan, m, y_out, o_ref, rx, sx, ry, sy, rz, sh, yb, own_share, send, recv, local):
    y, x, zh, tm = place()
    tms = [lax.rem(tm + d, NTM) for d in range(1, NTM)]
    greet(
        [device(y, x, zh, t) for t in tms]
        + [device(y, up(x, d), zh, tm) for d in (1, 2, 3)]
        + [device(up(y, d), x, zh, tm) for d in (1, 2, 3)]
        + [device(y, x, 1 - zh, tm)]
    )
    ox = [lax.rem(plan[b] // 2, 4) for b in range(SRC)]
    oy = [plan[b] // 8 for b in range(SRC)]
    oz = [lax.rem(plan[b], 2) for b in range(SRC)]
    my_lanes = pl.ds(pl.multiple_of(tm * KB, KB), KB)
    my_rows = pl.ds(pl.multiple_of(tm * SEG, SEG), SEG)

    def bins_of(t):
        return pl.ds(pl.multiple_of(t * KB, KB), KB)

    def main(first, count, base):
        return [
            remote(
                m.at[pl.ds(first, count), :, :, bins_of(tms[d - 1])],
                y_out.at[pl.ds(first, count), :, my_rows, :],
                send.at[base + d],
                recv.at[base + d],
                device(y, x, zh, tms[d - 1]),
            )
            for d in range(1, NTM)
        ]

    stage_x = []
    for d in (1, 3, 2):
        to = up(x, d)
        stage_x.append(
            remote(m.at[pl.ds(to * 8, 8)], rx.at[x], send.at[d], recv.at[d], device(y, to, zh, tm))
        )
    own_x = pltpu.make_async_copy(m.at[pl.ds(x * 8, 8)], rx.at[x], local.at[0])
    own_x.start()
    own_f = pltpu.make_async_copy(m.at[CH], sh.at[0], local.at[5])
    own_f.start()
    exchanged = main(0, EARLY, 8)
    own_m = pltpu.make_async_copy(
        m.at[pl.ds(0, CH), :, :, my_lanes], y_out.at[:, :, my_rows, :], local.at[1]
    )
    own_m.start()

    own_x.wait()
    for c in stage_x:
        c.wait_recv()
    for b in range(SRC):

        def pick_x(i, carry, b=b):
            sx[b, i] = rx[ox[b], i]
            return carry

        lax.fori_loop(0, 8, pick_x, 0)
    stage_y = []
    for d in (1, 3, 2):
        to = up(y, d)
        stage_y.append(
            remote(
                sx.at[:, pl.ds(to * 2, 2)],
                ry.at[y],
                send.at[4 + d],
                recv.at[4 + d],
                device(to, x, zh, tm),
            )
        )
    own_y = pltpu.make_async_copy(sx.at[:, pl.ds(y * 2, 2)], ry.at[y], local.at[2])
    own_y.start()
    own_y.wait()
    for c in stage_y:
        c.wait_recv()
    for b in range(SRC):

        def pick_y(i, carry, b=b):
            sy[i, b] = ry[oy[b], b, i]
            return carry

        lax.fori_loop(0, 2, pick_y, 0)
    stage_z = remote(sy.at[1 - zh], rz.at[zh], send.at[0], recv.at[0], device(y, x, 1 - zh, tm))
    own_z = pltpu.make_async_copy(sy.at[zh], rz.at[zh], local.at[3])
    own_z.start()
    own_z.wait()
    stage_z.wait_recv()
    own_f.wait()
    for b in range(SRC):
        sh[1 + b] = rz[oz[b], b]
    shares = [
        remote(
            sh.at[:, :, :, bins_of(tms[d - 1])],
            yb.at[:, :, my_rows, :],
            send.at[16 + d],
            recv.at[16 + d],
            device(y, x, zh, tms[d - 1]),
        )
        for d in range(1, NTM)
    ]
    own_s = pltpu.make_async_copy(sh.at[:, :, :, my_lanes], yb.at[:, :, my_rows, :], local.at[4])
    own_s.start()
    exchanged += main(EARLY, CH - EARLY, 24)
    own_s.wait()
    for c in shares:
        c.wait_recv()

    def turned(i, p):
        return yb[i, p].astype(jnp.float32).T

    for p in range(2):
        lanes = pl.ds(p * 128, 128)
        for b in range(SRC):
            own_share[pl.ds(b * KB, KB), lanes] = turned(1 + b, p).astype(jnp.bfloat16)
        own_share[pl.ds(SRC * KB, CH), lanes] = turned(0, p)[:CH].astype(jnp.bfloat16)

    cut = ROWS // 32 * 16
    me = y * 4 + x
    across = remote(
        own_share, o_ref.at[zh, me], send.at[32], recv.at[32], device(y, x, 1 - zh, tm)
    )
    own = pltpu.make_async_copy(own_share, o_ref.at[zh, me], local.at[6])
    own.start()
    started = []
    full, low, high = pl.ds(0, ROWS), pl.ds(0, cut), pl.ds(cut, ROWS - cut)

    class Half:
        def __init__(self, half):
            self.half = half
            ay, ax = half, 1 - half
            self.ap = device(up(y, ay), up(x, ax), zh, tm)
            self.am = device(up(y, 3 * ay), up(x, 3 * ax), zh, tm)
            self.bp = device(up(y, ax), up(x, ay), zh, tm)
            self.bm = device(up(y, 3 * ax), up(x, 3 * ay), zh, tm)
            self.a = x * ax + y * ay
            self.b = x * ay + y * ax
            self.base = 33 + 20 * half
            self.sent = {}
            self.passed = {}

        def put(self, b, a, part, k, where, source=None):
            slot = b * (4 - 3 * self.half) + a * (1 + 3 * self.half)
            ref = o_ref.at[self.half, slot, part]
            k = self.base + k
            copy = remote(ref if source is None else source, ref, send.at[k], recv.at[k], where)
            started.append(copy)
            return copy

        def at(self, r):
            return up(self.a, (0, 3, 1, 2)[r])

        def send_b(self, r, source=None):
            k = 4 + 4 * r
            self.sent[r] = (
                self.put(self.b, self.at(r), full, k, self.bp, source),
                self.put(self.b, self.at(r), full, k + 1, self.bm, source),
            )

        def start(self, source=None):
            self.a1 = self.put(self.b, self.a, full, 0, self.ap, source)
            self.a2 = self.put(self.b, self.a, full, 1, self.am, source)
            self.send_b(0, source)

        def first(self):
            self.a1.wait_recv()
            self.a3 = self.put(self.b, self.at(1), low, 2, self.ap)
            self.send_b(1)
            self.a2.wait_recv()
            self.a4 = self.put(self.b, self.at(2), high, 3, self.am)
            self.send_b(2)

        def second(self):
            self.a3.wait_recv()
            self.a4.wait_recv()
            self.send_b(3)

        def forward(self, r):
            k = 4 + 4 * r
            plus, minus = self.sent[r]
            plus.wait_recv()
            f1 = self.put(up(self.b, 3), self.at(r), low, k + 2, self.bp)
            minus.wait_recv()
            f2 = self.put(up(self.b, 1), self.at(r), high, k + 3, self.bm)
            self.passed[r] = (f1, f2)

    mine, other = Half(zh), Half(1 - zh)
    mine.start(own_share)
    mine.first()
    across.wait_recv()
    other.start()
    mine.forward(0)
    mine.second()
    other.first()
    mine.forward(1)
    other.forward(0)
    mine.forward(2)
    other.second()
    mine.forward(3)
    for r in (1, 2, 3):
        other.forward(r)
    for r in range(4):
        for h in (mine, other):
            for f in h.passed[r]:
                f.wait_recv()
    own.wait()
    own_m.wait()
    for c in exchanged:
        c.wait_recv()
    for c in stage_x + stage_y + [stage_z, across] + shares + exchanged + started:
        c.wait_send()


def front(plan, m):
    bf = jnp.bfloat16
    return pl.pallas_call(
        front_body,
        out_shape=(
            jax.ShapeDtypeStruct((CH, 2, NTM * SEG, KB), bf),
            jax.ShapeDtypeStruct((2, 16, ROWS, 256), bf),
        ),
        in_specs=[pl.BlockSpec(memory_space=pltpu.SMEM), pl.BlockSpec(memory_space=ANY)],
        out_specs=(pl.BlockSpec(memory_space=ANY), pl.BlockSpec(memory_space=ANY)),
        scratch_shapes=[
            pltpu.VMEM((4, 8, 2, SEG, BINS), bf),
            pltpu.VMEM((SRC, 8, 2, SEG, BINS), bf),
            pltpu.VMEM((4, SRC, 2, 2, SEG, BINS), bf),
            pltpu.VMEM((2, SRC, 2, SEG, BINS), bf),
            pltpu.VMEM((2, SRC, 2, SEG, BINS), bf),
            pltpu.VMEM((1 + SRC, 2, SEG, BINS), bf),
            pltpu.VMEM((1 + SRC, 2, NTM * SEG, KB), bf),
            pltpu.VMEM((ROWS, 256), bf),
            pltpu.SemaphoreType.DMA((73,)),
            pltpu.SemaphoreType.DMA((73,)),
            pltpu.SemaphoreType.DMA((7,)),
        ],
        compiler_params=pltpu.CompilerParams(
            collective_id=0, has_side_effects=True, vmem_limit_bytes=BIG
        ),
    )(plan, m)


def correlate_body(plan, g_ref, y_ref, out_ref, scale_ref, sa, sq, ra, rq, ob):
    f32, bf = jnp.float32, jnp.bfloat16

    def widen(j, carry):
        zh, y, x = lax.rem(j, 2), lax.rem(j // 2, 4), j // 8
        for b in range(SRC):
            rows = pl.ds(pl.multiple_of((b * CH + j) * KB, KB), KB)
            for p, part in enumerate((sa, sq)):
                lanes = pl.ds(p * 128, 128)
                part[rows, :] = g_ref[zh, y * 4 + x, pl.ds(b * KB, KB), lanes].astype(f32)
        rows = pl.ds(pl.multiple_of(j * KB, KB), KB)
        for p, part in enumerate((ra, rq)):
            part[rows, :] = y_ref[j, p].astype(f32).T
        return carry

    lax.fori_loop(0, CH, widen, 0)

    def flags(block):
        return g_ref[lax.rem(block, 2), block // 2, pl.ds(SRC * KB, CH), pl.ds(0, 128)]

    fr = flags(lax.axis_index("chan"))
    fr = jnp.concatenate([fr, fr], axis=0)
    counts = []
    for b in range(SRC):
        fs = flags(plan[b])
        counts.append(
            lax.dot_general(fs, fr, (((1,), (1,)), ((), ())), preferred_element_type=f32)
        )
    inverse = 1.0 / jnp.maximum(jnp.concatenate(counts, axis=0), 1.0)

    def one(k):
        sources, channels = pl.ds(k, SRC * CH, stride=KB), pl.ds(k, CH, stride=KB)
        s = jnp.concatenate([sa[sources, :], sq[sources, :]], axis=1).astype(bf)
        a, q = ra[channels, :], rq[channels, :]
        real, imag = jnp.concatenate([a, q], axis=1), jnp.concatenate([q, -a], axis=1)
        both = jnp.concatenate([real, imag], axis=0).astype(bf)
        res = lax.dot_general(s, both, (((1,), (1,)), ((), ())), preferred_element_type=f32)
        res = res * inverse
        ob[sources, :] = jnp.concatenate([res, jnp.zeros_like(res)], axis=1)

    def some(i, carry):
        for u in range(8):
            one(i * 8 + u)
        return carry

    lax.fori_loop(0, KB // 8, some, 0)

    def turn(t, carry):
        for i in range(12):
            s = t * 12 + i
            block = ob[pl.ds(pl.multiple_of(s * KB, KB), KB), pl.ds(0, 2 * CH)].T
            most = jnp.maximum(jnp.max(jnp.abs(block), axis=0, keepdims=True), 1e-30)
            code = jnp.round(block * (TOP / most)).astype(jnp.int32)
            out_ref[s] = code.astype(jnp.int16)
            scale_ref[t, pl.ds(i, 1), :] = most * (1.0 / TOP)
        return carry

    lax.fori_loop(0, NTM, turn, 0)


def correlate(plan, g, y):
    vmem = pl.BlockSpec(memory_space=pltpu.VMEM)
    return pl.pallas_call(
        correlate_body,
        out_shape=(
            jax.ShapeDtypeStruct((SRC * CH, 2 * CH, KB), jnp.int16),
            jax.ShapeDtypeStruct((NTM, 16, KB), jnp.float32),
        ),
        in_specs=[pl.BlockSpec(memory_space=pltpu.SMEM), vmem, vmem],
        out_specs=(vmem, vmem),
        scratch_shapes=[
            pltpu.VMEM((SRC * CH * KB, 128), jnp.float32),
            pltpu.VMEM((SRC * CH * KB, 128), jnp.float32),
            pltpu.VMEM((CH * KB, 128), jnp.float32),
            pltpu.VMEM((CH * KB, 128), jnp.float32),
            pltpu.VMEM((SRC * CH * KB, 128), jnp.float32),
        ],
        compiler_params=pltpu.CompilerParams(vmem_limit_bytes=BIG),
    )(plan, g, y)


def collect_body(x_ref, c_ref, v_ref, d_ref, send, recv, local):
    y, x, zh, tm = place()
    tms = [lax.rem(tm + d, NTM) for d in range(1, NTM)]
    greet([device(y, x, zh, t) for t in tms])
    copies = []
    for d in range(1, NTM):
        t = tms[d - 1]
        for i, (src, dst) in enumerate(((x_ref, v_ref), (c_ref, d_ref))):
            copies.append(
                remote(src.at[t], dst.at[tm], send.at[i, d], recv.at[i, d], device(y, x, zh, t))
            )
    own = [
        pltpu.make_async_copy(src.at[tm], dst.at[tm], local.at[i])
        for i, (src, dst) in enumerate(((x_ref, v_ref), (c_ref, d_ref)))
    ]
    for c in own:
        c.start()
    for c in own + copies:
        c.wait()


def collect(x, c):
    hbm = pl.BlockSpec(memory_space=ANY)
    return pl.pallas_call(
        collect_body,
        out_shape=(
            jax.ShapeDtypeStruct(x.shape, x.dtype),
            jax.ShapeDtypeStruct(c.shape, c.dtype),
        ),
        in_specs=[hbm, hbm],
        out_specs=(hbm, hbm),
        scratch_shapes=[
            pltpu.SemaphoreType.DMA((2, NTM)),
            pltpu.SemaphoreType.DMA((2, NTM)),
            pltpu.SemaphoreType.DMA((2,)),
        ],
        compiler_params=pltpu.CompilerParams(collective_id=2, has_side_effects=True),
    )(x, c)


def make_table():
    tau = lax.broadcasted_iota(jnp.int32, (1, 2 * BINS), 1) - BINS

    def pair(count, step):
        freq = lax.broadcasted_iota(jnp.int32, (count, 1), 0) * step
        angle = ((freq * tau) % (2 * BINS)).astype(jnp.float32) * (math.pi / BINS)
        return jnp.cos(angle), jnp.sin(angle)

    c1, s1 = (v[:, None, :] for v in pair(BINS // 8, 8))
    c2, s2 = (v[None, :, :] / math.sqrt(BINS) for v in pair(8, 1))
    shape = (BINS, 2 * BINS)
    table = jnp.concatenate(
        [(c1 * c2 - s1 * s2).reshape(shape), -(s1 * c2 + c1 * s2).reshape(shape)], axis=0
    )
    high = lax.reduce_precision(table, 8, 7)
    return high.astype(jnp.bfloat16), (table - high).astype(jnp.bfloat16)


def lags_body(v_ref, c_ref, th_ref, tl_ref, out_ref, xh, xl):
    @pl.when(pl.program_id(0) == 0)
    def _():
        def split(s, carry):
            rows = pl.ds(pl.multiple_of(s * CH, CH), CH)
            for p in range(2):
                for j in range(NTM):
                    lanes = pl.ds(p * BINS + j * KB, KB)
                    value = v_ref[j, s, p].astype(jnp.int32).astype(jnp.float32)
                    value = value * c_ref[j, pl.ds(s, 1), :]
                    high = value.astype(jnp.bfloat16)
                    xh[rows, lanes] = high
                    xl[rows, lanes] = (value - high.astype(jnp.float32)).astype(jnp.bfloat16)
            return carry

        lax.fori_loop(0, 12, split, 0)

    def dot(a, b):
        return jnp.dot(a, b, preferred_element_type=jnp.float32)

    th = th_ref[...]
    h = xh[...]
    out_ref[...] = dot(xl[...], th) + dot(h, tl_ref[...]) + dot(h, th)


def lags(v, c, th, tl):
    rows, wide, step = 12 * CH, 2 * BINS, 256
    return pl.pallas_call(
        lags_body,
        grid=(wide // step,),
        out_shape=jax.ShapeDtypeStruct((rows, wide), jnp.float32),
        in_specs=[
            pl.BlockSpec((NTM, 12, 2, CH, KB), lambda g: (0, 0, 0, 0, 0)),
            pl.BlockSpec((NTM, 16, KB), lambda g: (0, 0, 0)),
            pl.BlockSpec((wide, step), lambda g: (0, g)),
            pl.BlockSpec((wide, step), lambda g: (0, g)),
        ],
        out_specs=pl.BlockSpec((rows, step), lambda g: (0, g)),
        scratch_shapes=[
            pltpu.VMEM((rows, wide), jnp.bfloat16),
            pltpu.VMEM((rows, wide), jnp.bfloat16),
        ],
        compiler_params=pltpu.CompilerParams(vmem_limit_bytes=BIG),
    )(v, c, th, tl)


def shards(spectra, quality, plan):
    flags = quality.astype(jnp.bfloat16)
    masked = (spectra * flags[:, :, None, None]).transpose(0, 2, 1, 3)
    row = jnp.tile(jnp.pad(flags.T, ((0, 0), (0, KB - CH))), (1, NTM))
    m = jnp.concatenate([masked, jnp.broadcast_to(row, (1, 2, SEG, BINS))], axis=0)
    th, tl = make_table()
    y, g = front(plan, m)
    x, c = correlate(plan, g, y)
    v, c = collect(x.reshape(NTM, 12 * 2 * CH, KB), c)
    out = lags(v.reshape(NTM, 12, 2, CH, KB), c, th, tl)
    return out.reshape(12, CH, 2 * BINS)


def solution(mesh):
    in_specs = (P("chan", "tm", None, None), P("chan", "tm"), P())
    out_specs = P("tm", "chan", None)
    return jax.shard_map(shards, mesh=mesh, in_specs=in_specs, out_specs=out_specs, check_vma=False)
```

time: 258 us -> 224 us (0.87)
  Pallas kernels: 238 us -> 204 us
    pallas_call x5 -> x3, Pallas kernels: 221 us -> 188 us  [the longest x1 114 us: front(): pl.pallas_call(front_body, out_shape=(jax.ShapeDtypeStruct((CH, 2, NTM *...]
where the time goes in v2:
time: 224 us; the launch traced here: 220 us
  Pallas kernels  204 us (91%)
  other arithmetic  15.8 us (7%)
    pallas_call x1, Pallas kernels, front(): pl.pallas_call(front_body, out_shape=(jax.ShapeDtypeStruct((CH, 2, NTM *...  114 us
    pallas_call x1, Pallas kernels, collect(): pl.pallas_call(collect_body, out_shape=(jax.ShapeDtypeStruct(x.shape, x.d...  50.2 us
    pallas_call x1, Pallas kernels, correlate(): pl.pallas_call(correlate_body, out_shape=(jax.ShapeDtypeStruct((SRC * CH,...  23.7 us
    pallas_call x1, Pallas kernels, lags(): pl.pallas_call(lags_body, grid=(wide // step,), out_shape=jax.ShapeDtypeS...  15.9 us
    convert_element_type x1, other arithmetic, make_table(): return (high.astype(jnp.bfloat16), (table - high).astype(jnp.bfloat16))  7.03 us

profile of v2, /device:TPU:225, one launch (start us, length us, event | category | flops | bytes accessed | tf_op | source)
XLA Modules:
  0.0 220.3 jit_solution(9853893390262450683)
XLA Ops:
  0.0 4.1 %fusion.6 = (f32[128,2048]{1,0:T(8,128)S(1)}, f32[128,2048]{1,0:T(8,128)S(1)}) fusion(s32[2048]{0:T(1024)S(1)} %iota_add_fusion, s32[128]{0:T(128)S(1)} %iota_multiply_fusion), kind=kLoop, calls=%fused_computation.18 | loop fusion | flops 3670016 | bytes 2105856 | tf_op jit(solution)/shard_map/cos | solution.py:420
  4.1 0.3 cosine_multiply_fusion
  4.4 2.5 %subtract_bitcast_fusion = (f32[1024,2048]{1,0:T(8,128)S(1)}, f32[1024,2048]{1,0:T(8,128)S(1)}) fusion(f32[8,2048]{1,0:T(8,128)S(1)} %get-tuple-element.24, f32[128,2048]{1,0:T(8,128)S(1)} %get-tuple-element.22, f32[8,2048]{1,0:T(8,128)S(1)} %get-tuple-element.23, f32[128,2048]{1,0:T(8,128)S(1)} %get-tuple-element.21), kind=kLoop, calls=%fused_computation.5 | loop fusion | flops 14680064 | bytes 19005440 | tf_op jit(solution)/shard_map/sub | solution.py:426
  6.9 0.0 copy-start.1
  6.9 0.0 copy-start
  6.9 7.0 %fusion = (bf16[2048,2048]{1,0:T(8,128)(2,1)}, bf16[2048,2048]{1,0:T(8,128)(2,1)}) fusion(f32[1024,2048]{1,0:T(8,128)S(1)} %get-tuple-element.20, f32[1024,2048]{1,0:T(8,128)S(1)} %get-tuple-element.19), kind=kLoop, calls=%fused_computation.2 | loop fusion | flops 20971520 | bytes 33554432 | tf_op jit(solution)/shard_map/convert_element_type | solution.py:429
  14.0 0.0 copy-done.1
  14.0 0.1 copy.4
  14.1 0.0 copy-done
  14.1 0.4 fusion.1
  14.5 1.5 pad_maximum_fusion.1.m
  16.0 114.4 %shard_map.37 = (bf16[32,2,128,128]{3,2,1,0:T(8,128)(2,1)}, bf16[2,16,416,256]{3,2,1,0:T(8,128)(2,1)}) custom-call(s32[3]{0:T(128)} %plan.3, bf16[33,2,16,1024]{3,2,1,0:T(8,128)(2,1)} %pad_maximum_fusion.1.m), custom_call_target="tpu_custom_call" | custom-call | tf_op jit(solution)/shard_map/pallas_call | solution.py:266
  130.4 23.7 %shard_map.38 = (s16[96,64,128]{2,1,0:T(8,128)(2,1)}, f32[8,16,128]{2,1,0:T(8,128)}) custom-call(s32[3]{0:T(128)} %plan.3, bf16[2,16,416,256]{3,2,1,0:T(8,128)(2,1)} %get-tuple-element.11.g_ref, bf16[32,2,128,128]{3,2,1,0:T(8,128)(2,1)} %get-tuple-element.12.y_ref), custom_call_target="tpu_custom_call" | custom-call | tf_op jit(solution)/shard_map/pallas_call | solution.py:355
  154.1 50.2 %shard_map.39 = (s16[8,768,128]{2,1,0:T(8,128)(2,1)}, f32[8,16,128]{2,1,0:T(8,128)}) custom-call(s16[8,768,128]{2,1,0:T(8,128)(2,1)} %bitcast.15, f32[8,16,128]{2,1,0:T(8,128)} %get-tuple-element.14.c_ref), custom_call_target="tpu_custom_call" | custom-call | tf_op jit(solution)/shard_map/pallas_call | solution.py:397
  204.3 15.9 %shard_map.40 = f32[384,2048]{1,0:T(8,128)} custom-call(s16[8,12,2,32,128]{4,3,2,1,0:T(8,128)(2,1)} %bitcast.16, f32[8,16,128]{2,1,0:T(8,128)} %get-tuple-element.16.c_ref, bf16[2048,2048]{1,0:T(8,128)(2,1)} %get-tuple-element.18.th_ref, bf16[2048,2048]{1,0:T(8,128)(2,1)} %get-tuple-element.17.tl_ref), custom_call_target="tpu_custom_call" | custom-call | tf_op jit(solution)/shard_map/pallas_call | solution.py:459
  (8 shorter events, 0.0 us)
Async XLA Ops:
  6.9 7.1 %copy-start.1 = (s32[32,16]{0,1:T(8,128)S(1)}, s32[32,16]{0,1:T(8,128)}, u32[]{:S(2)}) copy-start(s32[32,16]{0,1:T(8,128)} %param.4) | copy-start | bytes 6148
  6.9 7.1 %copy-start = (bf16[32,16,2,1024]{3,2,1,0:T(2,128)(2,1)S(1)}, bf16[32,16,2,1024]{3,2,1,0:T(2,128)(2,1)}, u32[]{:S(2)}) copy-start(bf16[32,16,2,1024]{3,2,1,0:T(2,128)(2,1)} %param.3) | copy-start | bytes 6291460

commit v3 on v2

--- a/solution.py
+++ b/solution.py
@@ -51,7 +51,7 @@
     return copy
 
 
-def front_body(plan, m, y_out, o_ref, rx, sx, ry, sy, rz, sh, yb, own_share, send, recv, local):
+def front_body(plan, m, y_out, o_ref, r1, s1, r2, s2, rz, sh, yb, own_share, send, recv, local):
     y, x, zh, tm = place()
     tms = [lax.rem(tm + d, NTM) for d in range(1, NTM)]
     greet(
@@ -81,58 +81,86 @@
             for d in range(1, NTM)
         ]
 
-    stage_x = []
+    def first_to(h, d):
+        return (y, up(x, d)) if h == 0 else (up(y, d), x)
+
+    def second_to(h, d):
+        return first_to(1 - h, d)
+
+    first_at, second_at = (x, y), (y, x)
+    first_owner, second_owner = (ox, oy), (oy, ox)
+    stage_1 = []
     for d in (1, 3, 2):
-        to = up(x, d)
-        stage_x.append(
-            remote(m.at[pl.ds(to * 8, 8)], rx.at[x], send.at[d], recv.at[d], device(y, to, zh, tm))
+        for h in range(2):
+            to = first_to(h, d)
+            piece = pl.ds(16 * h + 4 * up(first_at[h], d), 4)
+            stage_1.append(
+                remote(
+                    m.at[piece],
+                    r1.at[h, first_at[h]],
+                    send.at[3 * h + d],
+                    recv.at[3 * h + d],
+                    device(*to, zh, tm),
+                )
+            )
+    own_1 = [
+        pltpu.make_async_copy(
+            m.at[pl.ds(16 * h + 4 * first_at[h], 4)], r1.at[h, first_at[h]], local.at[7 + h]
         )
-    own_x = pltpu.make_async_copy(m.at[pl.ds(x * 8, 8)], rx.at[x], local.at[0])
-    own_x.start()
+        for h in range(2)
+    ]
+    for c in own_1:
+        c.start()
     own_f = pltpu.make_async_copy(m.at[CH], sh.at[0], local.at[5])
     own_f.start()
-    exchanged = main(0, EARLY, 8)
+    exchanged = main(0, EARLY, 73)
     own_m = pltpu.make_async_copy(
         m.at[pl.ds(0, CH), :, :, my_lanes], y_out.at[:, :, my_rows, :], local.at[1]
     )
     own_m.start()
 
-    own_x.wait()
-    for c in stage_x:
+    for c in own_1:
+        c.wait()
+    for c in stage_1:
         c.wait_recv()
-    for b in range(SRC):
-
-        def pick_x(i, carry, b=b):
-            sx[b, i] = rx[ox[b], i]
-            return carry
-
-        lax.fori_loop(0, 8, pick_x, 0)
-    stage_y = []
+    for h in range(2):
+        for b in range(SRC):
+
+            def pick(i, carry, h=h, b=b):
+                s1[h, b, i] = r1[h, first_owner[h][b], i]
+                return carry
+
+            lax.fori_loop(0, 4, pick, 0)
+    stage_2 = []
     for d in (1, 3, 2):
-        to = up(y, d)
-        stage_y.append(
-            remote(
-                sx.at[:, pl.ds(to * 2, 2)],
-                ry.at[y],
-                send.at[4 + d],
-                recv.at[4 + d],
-                device(to, x, zh, tm),
+        for h in range(2):
+            to = second_to(h, d)
+            stage_2.append(
+                remote(
+                    s1.at[h, :, up(second_at[h], d)],
+                    r2.at[h, second_at[h]],
+                    send.at[6 + 3 * h + d],
+                    recv.at[6 + 3 * h + d],
+                    device(*to, zh, tm),
+                )
             )
+    own_2 = [
+        pltpu.make_async_copy(
+            s1.at[h, :, second_at[h]], r2.at[h, second_at[h]], local.at[2 * h]
         )
-    own_y = pltpu.make_async_copy(sx.at[:, pl.ds(y * 2, 2)], ry.at[y], local.at[2])
-    own_y.start()
-    own_y.wait()
-    for c in stage_y:
+        for h in range(2)
+    ]
+    for c in own_2:
+        c.start()
+    for c in own_2:
+        c.wait()
+    for c in stage_2:
         c.wait_recv()
-    for b in range(SRC):
-
-        def pick_y(i, carry, b=b):
-            sy[i, b] = ry[oy[b], b, i]
-            return carry
-
-        lax.fori_loop(0, 2, pick_y, 0)
-    stage_z = remote(sy.at[1 - zh], rz.at[zh], send.at[0], recv.at[0], device(y, x, 1 - zh, tm))
-    own_z = pltpu.make_async_copy(sy.at[zh], rz.at[zh], local.at[3])
+    for h in range(2):
+        for b in range(SRC):
+            s2[h, b] = r2[h, second_owner[h][b], b]
+    stage_z = remote(s2.at[1 - zh], rz.at[zh], send.at[0], recv.at[0], device(y, x, 1 - zh, tm))
+    own_z = pltpu.make_async_copy(s2.at[zh], rz.at[zh], local.at[3])
     own_z.start()
     own_z.wait()
     stage_z.wait_recv()
@@ -257,7 +285,7 @@
     own_m.wait()
     for c in exchanged:
         c.wait_recv()
-    for c in stage_x + stage_y + [stage_z, across] + shares + exchanged + started:
+    for c in stage_1 + stage_2 + [stage_z, across] + shares + exchanged + started:
         c.wait_send()
 
 
@@ -272,17 +300,17 @@
         in_specs=[pl.BlockSpec(memory_space=pltpu.SMEM), pl.BlockSpec(memory_space=ANY)],
         out_specs=(pl.BlockSpec(memory_space=ANY), pl.BlockSpec(memory_space=ANY)),
         scratch_shapes=[
-            pltpu.VMEM((4, 8, 2, SEG, BINS), bf),
-            pltpu.VMEM((SRC, 8, 2, SEG, BINS), bf),
-            pltpu.VMEM((4, SRC, 2, 2, SEG, BINS), bf),
+            pltpu.VMEM((2, 4, 4, 2, SEG, BINS), bf),
+            pltpu.VMEM((2, SRC, 4, 2, SEG, BINS), bf),
+            pltpu.VMEM((2, 4, SRC, 2, SEG, BINS), bf),
             pltpu.VMEM((2, SRC, 2, SEG, BINS), bf),
             pltpu.VMEM((2, SRC, 2, SEG, BINS), bf),
             pltpu.VMEM((1 + SRC, 2, SEG, BINS), bf),
             pltpu.VMEM((1 + SRC, 2, NTM * SEG, KB), bf),
             pltpu.VMEM((ROWS, 256), bf),
-            pltpu.SemaphoreType.DMA((73,)),
-            pltpu.SemaphoreType.DMA((73,)),
-            pltpu.SemaphoreType.DMA((7,)),
+            pltpu.SemaphoreType.DMA((81,)),
+            pltpu.SemaphoreType.DMA((81,)),
+            pltpu.SemaphoreType.DMA((9,)),
         ],
         compiler_params=pltpu.CompilerParams(
             collective_id=0, has_side_effects=True, vmem_limit_bytes=BIG
@@ -294,12 +322,13 @@
     f32, bf = jnp.float32, jnp.bfloat16
 
     def widen(j, carry):
-        zh, y, x = lax.rem(j, 2), lax.rem(j // 2, 4), j // 8
+        zh, a, c = j // 16, lax.rem(j // 4, 4), lax.rem(j, 4)
+        slot = c * (4 - 3 * zh) + a * (1 + 3 * zh)
         for b in range(SRC):
             rows = pl.ds(pl.multiple_of((b * CH + j) * KB, KB), KB)
             for p, part in enumerate((sa, sq)):
                 lanes = pl.ds(p * 128, 128)
-                part[rows, :] = g_ref[zh, y * 4 + x, pl.ds(b * KB, KB), lanes].astype(f32)
+                part[rows, :] = g_ref[zh, slot, pl.ds(b * KB, KB), lanes].astype(f32)
         rows = pl.ds(pl.multiple_of(j * KB, KB), KB)
         for p, part in enumerate((ra, rq)):
             part[rows, :] = y_ref[j, p].astype(f32).T
@@ -320,7 +349,7 @@
         )
     inverse = 1.0 / jnp.maximum(jnp.concatenate(counts, axis=0), 1.0)
 
-    def one(k):
+    def one(k, to):
         sources, channels = pl.ds(k, SRC * CH, stride=KB), pl.ds(k, CH, stride=KB)
         s = jnp.concatenate([sa[sources, :], sq[sources, :]], axis=1).astype(bf)
         a, q = ra[channels, :], rq[channels, :]
@@ -328,11 +357,11 @@
         both = jnp.concatenate([real, imag], axis=0).astype(bf)
         res = lax.dot_general(s, both, (((1,), (1,)), ((), ())), preferred_element_type=f32)
         res = res * inverse
-        ob[sources, :] = jnp.concatenate([res, jnp.zeros_like(res)], axis=1)
+        ob[pl.ds(to, SRC * CH, stride=KB), :] = jnp.concatenate([res, jnp.zeros_like(res)], axis=1)
 
     def some(i, carry):
         for u in range(8):
-            one(i * 8 + u)
+            one(i * 8 + u, i * 4 + u // 2 + u % 2 * (KB // 2))
         return carry
 
     lax.fori_loop(0, KB // 8, some, 0)
@@ -371,7 +400,9 @@
     )(plan, g, y)
 
 
-def collect_body(x_ref, c_ref, v_ref, d_ref, send, recv, local):
+def collect_body(
+    x_ref, c_ref, c1, s1, c2, s2, v_ref, d_ref, th_ref, tl_ref, th, tl, send, recv, local
+):
     y, x, zh, tm = place()
     tms = [lax.rem(tm + d, NTM) for d in range(1, NTM)]
     greet([device(y, x, zh, t) for t in tms])
@@ -388,60 +419,97 @@
     ]
     for c in own:
         c.start()
-    for c in own + copies:
+
+    def make(e1, carry):
+        cos1 = jnp.broadcast_to(c1[pl.ds(e1, 1), :], (16, BINS))
+        sin1 = jnp.broadcast_to(s1[pl.ds(e1, 1), :], (16, BINS))
+        for parity in range(2):
+            cos = cos1 * c2[parity] - sin1 * s2[parity]
+            sin = -(sin1 * c2[parity] + cos1 * s2[parity])
+            for p, value in enumerate((cos, sin)):
+                high = value.astype(jnp.bfloat16)
+                low = (value - high.astype(jnp.float32)).astype(jnp.bfloat16)
+                th[parity, p, e1] = high
+                tl[parity, p, e1] = low
+        return carry
+
+    lax.fori_loop(0, BINS // 32, make, 0)
+    out = [
+        pltpu.make_async_copy(th, th_ref, local.at[2]),
+        pltpu.make_async_copy(tl, tl_ref, local.at[3]),
+    ]
+    for c in out:
+        c.start()
+    for c in own + copies + out:
         c.wait()
 
 
-def collect(x, c):
-    hbm = pl.BlockSpec(memory_space=ANY)
+def collect(x, c, seeds):
+    hbm, vmem = pl.BlockSpec(memory_space=ANY), pl.BlockSpec(memory_space=pltpu.VMEM)
+    table = (2, 2, BINS // 32, 16, BINS)
     return pl.pallas_call(
         collect_body,
         out_shape=(
             jax.ShapeDtypeStruct(x.shape, x.dtype),
             jax.ShapeDtypeStruct(c.shape, c.dtype),
+            jax.ShapeDtypeStruct(table, jnp.bfloat16),
+            jax.ShapeDtypeStruct(table, jnp.bfloat16),
         ),
-        in_specs=[hbm, hbm],
-        out_specs=(hbm, hbm),
+        in_specs=[hbm, hbm, vmem, vmem, vmem, vmem],
+        out_specs=(hbm, hbm, hbm, hbm),
         scratch_shapes=[
+            pltpu.VMEM(table, jnp.bfloat16),
+            pltpu.VMEM(table, jnp.bfloat16),
             pltpu.SemaphoreType.DMA((2, NTM)),
             pltpu.SemaphoreType.DMA((2, NTM)),
-            pltpu.SemaphoreType.DMA((2,)),
+            pltpu.SemaphoreType.DMA((4,)),
         ],
-        compiler_params=pltpu.CompilerParams(collective_id=2, has_side_effects=True),
-    )(x, c)
-
-
-def make_table():
-    tau = lax.broadcasted_iota(jnp.int32, (1, 2 * BINS), 1) - BINS
-
-    def pair(count, step):
-        freq = lax.broadcasted_iota(jnp.int32, (count, 1), 0) * step
+        compiler_params=pltpu.CompilerParams(
+            collective_id=2, has_side_effects=True, vmem_limit_bytes=BIG
+        ),
+    )(x, c, *seeds)
+
+
+def make_seeds():
+    tau = lax.broadcasted_iota(jnp.int32, (1, BINS), 1)
+
+    def pair(freq):
         angle = ((freq * tau) % (2 * BINS)).astype(jnp.float32) * (math.pi / BINS)
         return jnp.cos(angle), jnp.sin(angle)
 
-    c1, s1 = (v[:, None, :] for v in pair(BINS // 8, 8))
-    c2, s2 = (v[None, :, :] / math.sqrt(BINS) for v in pair(8, 1))
-    shape = (BINS, 2 * BINS)
-    table = jnp.concatenate(
-        [(c1 * c2 - s1 * s2).reshape(shape), -(s1 * c2 + c1 * s2).reshape(shape)], axis=0
+    c1, s1 = pair(lax.broadcasted_iota(jnp.int32, (BINS // 32, 1), 0) * 32)
+    row = lax.broadcasted_iota(jnp.int32, (32, 1), 0)
+    c2, s2 = (
+        (v / math.sqrt(BINS)).reshape(2, 16, BINS) for v in pair(row % 16 * 2 + row // 16)
     )
-    high = lax.reduce_precision(table, 8, 7)
-    return high.astype(jnp.bfloat16), (table - high).astype(jnp.bfloat16)
+    return c1, s1, c2, s2
 
 
 def lags_body(v_ref, c_ref, th_ref, tl_ref, out_ref, xh, xl):
+    step = th_ref.shape[2]
+
     @pl.when(pl.program_id(0) == 0)
     def _():
+        lane = lax.broadcasted_iota(jnp.int32, (CH, KB), 1)
+
         def split(s, carry):
             rows = pl.ds(pl.multiple_of(s * CH, CH), CH)
             for p in range(2):
-                for j in range(NTM):
-                    lanes = pl.ds(p * BINS + j * KB, KB)
-                    value = v_ref[j, s, p].astype(jnp.int32).astype(jnp.float32)
-                    value = value * c_ref[j, pl.ds(s, 1), :]
-                    high = value.astype(jnp.bfloat16)
-                    xh[rows, lanes] = high
-                    xl[rows, lanes] = (value - high.astype(jnp.float32)).astype(jnp.bfloat16)
+                for j in range(NTM // 2):
+                    a, b = (
+                        v_ref[2 * j + i, s, p].astype(jnp.int32).astype(jnp.float32)
+                        * c_ref[2 * j + i, pl.ds(s, 1), :]
+                        for i in range(2)
+                    )
+                    even = jnp.where(lane < KB // 2, a, pltpu.roll(b, KB // 2, 1))
+                    odd = jnp.where(lane < KB // 2, pltpu.roll(a, KB // 2, 1), b)
+                    lanes = pl.ds(p * (BINS // 2) + j * KB, KB)
+                    for parity, value in enumerate((even, odd)):
+                        high = value.astype(jnp.bfloat16)
+                        xh[parity, rows, lanes] = high
+                        xl[parity, rows, lanes] = (value - high.astype(jnp.float32)).astype(
+                            jnp.bfloat16
+                        )
             return carry
 
         lax.fori_loop(0, 12, split, 0)
@@ -449,27 +517,30 @@
     def dot(a, b):
         return jnp.dot(a, b, preferred_element_type=jnp.float32)
 
-    th = th_ref[...]
-    h = xh[...]
-    out_ref[...] = dot(xl[...], th) + dot(h, tl_ref[...]) + dot(h, th)
+    even, odd = (
+        dot(xl[i], th_ref[i]) + dot(xh[i], tl_ref[i]) + dot(xh[i], th_ref[i]) for i in range(2)
+    )
+    at = pl.program_id(0) * step
+    out_ref[:, pl.ds(pl.multiple_of(at, step), step)] = even - odd
+    out_ref[:, pl.ds(pl.multiple_of(at + BINS, step), step)] = even + odd
 
 
 def lags(v, c, th, tl):
-    rows, wide, step = 12 * CH, 2 * BINS, 256
+    rows, step = 12 * CH, 256
     return pl.pallas_call(
         lags_body,
-        grid=(wide // step,),
-        out_shape=jax.ShapeDtypeStruct((rows, wide), jnp.float32),
+        grid=(BINS // step,),
+        out_shape=jax.ShapeDtypeStruct((rows, 2 * BINS), jnp.float32),
         in_specs=[
             pl.BlockSpec((NTM, 12, 2, CH, KB), lambda g: (0, 0, 0, 0, 0)),
             pl.BlockSpec((NTM, 16, KB), lambda g: (0, 0, 0)),
-            pl.BlockSpec((wide, step), lambda g: (0, g)),
-            pl.BlockSpec((wide, step), lambda g: (0, g)),
+            pl.BlockSpec((2, BINS, step), lambda g: (0, 0, g)),
+            pl.BlockSpec((2, BINS, step), lambda g: (0, 0, g)),
         ],
-        out_specs=pl.BlockSpec((rows, step), lambda g: (0, g)),
+        out_specs=pl.BlockSpec((rows, 2 * BINS), lambda g: (0, 0)),
         scratch_shapes=[
-            pltpu.VMEM((rows, wide), jnp.bfloat16),
-            pltpu.VMEM((rows, wide), jnp.bfloat16),
+            pltpu.VMEM((2, rows, BINS), jnp.bfloat16),
+            pltpu.VMEM((2, rows, BINS), jnp.bfloat16),
         ],
         compiler_params=pltpu.CompilerParams(vmem_limit_bytes=BIG),
     )(v, c, th, tl)
@@ -480,10 +551,10 @@
     masked = (spectra * flags[:, :, None, None]).transpose(0, 2, 1, 3)
     row = jnp.tile(jnp.pad(flags.T, ((0, 0), (0, KB - CH))), (1, NTM))
     m = jnp.concatenate([masked, jnp.broadcast_to(row, (1, 2, SEG, BINS))], axis=0)
-    th, tl = make_table()
     y, g = front(plan, m)
     x, c = correlate(plan, g, y)
-    v, c = collect(x.reshape(NTM, 12 * 2 * CH, KB), c)
+    v, c, th, tl = collect(x.reshape(NTM, 12 * 2 * CH, KB), c, make_seeds())
+    th, tl = (t.reshape(2, BINS, BINS) for t in (th, tl))
     out = lags(v.reshape(NTM, 12, 2, CH, KB), c, th, tl)
     return out.reshape(12, CH, 2 * BINS)
 

time: 224 us -> 197 us (0.88)
  Pallas kernels: 204 us -> 185 us
  other arithmetic: 15.8 us -> 7.52 us
    pallas_call x1, Pallas kernels: 114 us -> 105 us  [front(): pl.pallas_call(front_body, out_shape=(jax.ShapeDtypeStruct((CH, 2, NTM *...]
    convert_element_type x1 -> x0, other arithmetic: 7.03 us -> none  [make_table(): return (high.astype(jnp.bfloat16), (table - high).astype(jnp.bfloat16))]
    pallas_call x1, Pallas kernels: 50.2 us -> 43.6 us  [collect(): pl.pallas_call(collect_body, out_shape=(jax.ShapeDtypeStruct(x.shape, x.d...]
    pallas_call x1, Pallas kernels: 15.9 us -> 11.4 us  [lags(): pl.pallas_call(lags_body, grid=(BINS // step,), out_shape=jax.ShapeDtypeS...]
    cos x1 -> x0, other arithmetic: 4.13 us -> none  [pair(): return (jnp.cos(angle), jnp.sin(angle))]
    sub x2 -> x0, other arithmetic: 2.47 us -> none  [the longest x1 2.47 us: make_table(): c1 * c2 - s1 * s2]
where the time goes in v3:
time: 197 us; the launch traced here: 193 us
  Pallas kernels  185 us (94%)
  other arithmetic  7.52 us (4%)
    pallas_call x1, Pallas kernels, front(): pl.pallas_call(front_body, out_shape=(jax.ShapeDtypeStruct((CH, 2, NTM *...  105 us
    pallas_call x1, Pallas kernels, collect(): pl.pallas_call(collect_body, out_shape=(jax.ShapeDtypeStruct(x.shape, x.d...  43.6 us
    pallas_call x1, Pallas kernels, correlate(): pl.pallas_call(correlate_body, out_shape=(jax.ShapeDtypeStruct((SRC * CH,...  25.9 us
    pallas_call x1, Pallas kernels, lags(): pl.pallas_call(lags_body, grid=(BINS // step,), out_shape=jax.ShapeDtypeS...  11.4 us

profile of v3, /device:TPU:225, one launch (start us, length us, event | category | flops | bytes accessed | tf_op | source)
XLA Modules:
  0.0 193.1 jit_solution(14232402367483088630)
XLA Ops:
  0.0 0.7 convert_bitcast_fusion
  0.7 0.7 convert_element_type.17
  1.4 0.1 copy.4
  1.6 1.3 sine_multiply_fusion
  2.9 1.3 fusion.13
  4.2 2.0 %fusion = bf16[32,2,16,1024]{3,2,1,0:T(8,128)(2,1)S(1)} fusion(bf16[32,16,2,1024]{3,2,1,0:T(2,128)(2,1)} %param.3, bf16[32,16]{1,0:T(8,128)(2,1)S(1)} %copy.4), kind=kLoop, calls=%fused_computation.2 | loop fusion | flops 1048576 | bytes 4195328 | tf_op jit(solution)/shard_map/transpose | solution.py:551
  6.1 1.5 pad_maximum_fusion.m
  7.7 104.6 %shard_map.37 = (bf16[32,2,128,128]{3,2,1,0:T(8,128)(2,1)}, bf16[2,16,416,256]{3,2,1,0:T(8,128)(2,1)}) custom-call(s32[3]{0:T(128)} %plan.3, bf16[33,2,16,1024]{3,2,1,0:T(8,128)(2,1)} %pad_maximum_fusion.m), custom_call_target="tpu_custom_call" | custom-call | tf_op jit(solution)/shard_map/pallas_call | solution.py:294
  112.3 25.9 %shard_map.38 = (s16[96,64,128]{2,1,0:T(8,128)(2,1)}, f32[8,16,128]{2,1,0:T(8,128)}) custom-call(s32[3]{0:T(128)} %plan.3, bf16[2,16,416,256]{3,2,1,0:T(8,128)(2,1)} %get-tuple-element.13.g_ref, bf16[32,2,128,128]{3,2,1,0:T(8,128)(2,1)} %get-tuple-element.14.y_ref), custom_call_target="tpu_custom_call" | custom-call | tf_op jit(solution)/shard_map/pallas_call | solution.py:384
  138.1 43.6 %shard_map.39 = (s16[8,768,128]{2,1,0:T(8,128)(2,1)}, f32[8,16,128]{2,1,0:T(8,128)}, bf16[2,2,32,16,1024]{4,3,2,1,0:T(8,128)(2,1)}, bf16[2,2,32,16,1024]{4,3,2,1,0:T(8,128)(2,1)}) custom-call(s16[8,768,128]{2,1,0:T(8,128)(2,1)} %bitcast.16, f32[8,16,128]{2,1,0:T(8,128)} %get-tuple-element.16.c_ref, f32[32,1024]{1,0:T(8,128)} %get-tuple-element.24.c1, ...), custom_call_target="tpu_custom_call" | custom-call | tf_op jit(solution)/shard_map/pallas_call | solution.py:450
  181.7 11.4 %shard_map.40 = f32[384,2048]{1,0:T(8,128)} custom-call(s16[8,12,2,32,128]{4,3,2,1,0:T(8,128)(2,1)} %bitcast.15, f32[8,16,128]{2,1,0:T(8,128)} %get-tuple-element.18.c_ref, bf16[2,1024,1024]{2,1,0:T(8,128)(2,1)} %bitcast.13, bf16[2,1024,1024]{2,1,0:T(8,128)(2,1)} %bitcast.14), custom_call_target="tpu_custom_call" | custom-call | tf_op jit(solution)/shard_map/pallas_call | solution.py:530
  (6 shorter events, 0.0 us)

commit v4 on v3

--- a/solution.py
+++ b/solution.py
@@ -7,6 +7,7 @@
 from jax.experimental import pallas as pl
 from jax.experimental.pallas import tpu as pltpu
 from jax.sharding import PartitionSpec as P
+import numpy as np
 
 MESH = pl.DeviceIdType.MESH
 ANY = pl.ANY
@@ -17,7 +18,7 @@
 SEG = 16
 BINS = 1024
 KB = BINS // NTM
-ROWS = SRC * KB + CH
+ROWS = SRC * KB + CH // 2
 EARLY = 16
 TOP = 32766.0
 BIG = 56 * 1024 * 1024
@@ -51,14 +52,14 @@
     return copy
 
 
-def front_body(plan, m, y_out, o_ref, r1, s1, r2, s2, rz, sh, yb, own_share, send, recv, local):
+def front_body(plan, m, y_out, o_ref, r1, s1, r2, s2, fb, yb, own_share, send, recv, local):
     y, x, zh, tm = place()
     tms = [lax.rem(tm + d, NTM) for d in range(1, NTM)]
     greet(
         [device(y, x, zh, t) for t in tms]
         + [device(y, up(x, d), zh, tm) for d in (1, 2, 3)]
         + [device(up(y, d), x, zh, tm) for d in (1, 2, 3)]
-        + [device(y, x, 1 - zh, tm)]
+        + [device(y, x, 1 - zh, t) for t in tms + [tm]]
     )
     ox = [lax.rem(plan[b] // 2, 4) for b in range(SRC)]
     oy = [plan[b] // 8 for b in range(SRC)]
@@ -111,7 +112,17 @@
     ]
     for c in own_1:
         c.start()
-    own_f = pltpu.make_async_copy(m.at[CH], sh.at[0], local.at[5])
+    flags = [
+        remote(
+            m.at[CH, 0, :, bins_of(t)],
+            fb.at[my_rows, :],
+            send.at[24 + d],
+            recv.at[24 + d],
+            device(y, x, zh, t),
+        )
+        for d, t in enumerate(tms, 1)
+    ]
+    own_f = pltpu.make_async_copy(m.at[CH, 0, :, my_lanes], fb.at[my_rows, :], local.at[5])
     own_f.start()
     exchanged = main(0, EARLY, 73)
     own_m = pltpu.make_async_copy(
@@ -159,39 +170,39 @@
     for h in range(2):
         for b in range(SRC):
             s2[h, b] = r2[h, second_owner[h][b], b]
-    stage_z = remote(s2.at[1 - zh], rz.at[zh], send.at[0], recv.at[0], device(y, x, 1 - zh, tm))
-    own_z = pltpu.make_async_copy(s2.at[zh], rz.at[zh], local.at[3])
-    own_z.start()
-    own_z.wait()
-    stage_z.wait_recv()
+    shares = []
+    for other in range(2):
+        half = zh + other * (1 - 2 * zh)
+        for d in range(1 - other, NTM):
+            t = lax.rem(tm + d, NTM)
+            k = 81 + 8 * other + d
+            shares.append(
+                remote(
+                    s2.at[half, :, :, :, bins_of(t)],
+                    yb.at[zh, :, :, my_rows, :],
+                    send.at[k],
+                    recv.at[k],
+                    device(y, x, half, t),
+                )
+            )
+    own_s = pltpu.make_async_copy(
+        s2.at[zh, :, :, :, my_lanes], yb.at[zh, :, :, my_rows, :], local.at[4]
+    )
+    own_s.start()
+    exchanged += main(EARLY, CH - EARLY, 15)
+    own_s.wait()
     own_f.wait()
-    for b in range(SRC):
-        sh[1 + b] = rz[oz[b], b]
-    shares = [
-        remote(
-            sh.at[:, :, :, bins_of(tms[d - 1])],
-            yb.at[:, :, my_rows, :],
-            send.at[16 + d],
-            recv.at[16 + d],
-            device(y, x, zh, tms[d - 1]),
-        )
-        for d in range(1, NTM)
-    ]
-    own_s = pltpu.make_async_copy(sh.at[:, :, :, my_lanes], yb.at[:, :, my_rows, :], local.at[4])
-    own_s.start()
-    exchanged += main(EARLY, CH - EARLY, 24)
-    own_s.wait()
-    for c in shares:
+    for c in flags + shares:
         c.wait_recv()
-
-    def turned(i, p):
-        return yb[i, p].astype(jnp.float32).T
 
     for p in range(2):
         lanes = pl.ds(p * 128, 128)
         for b in range(SRC):
-            own_share[pl.ds(b * KB, KB), lanes] = turned(1 + b, p).astype(jnp.bfloat16)
-        own_share[pl.ds(SRC * KB, CH), lanes] = turned(0, p)[:CH].astype(jnp.bfloat16)
+            part = yb[oz[b], b, p].astype(jnp.float32).T
+            own_share[pl.ds(b * KB, KB), lanes] = part.astype(jnp.bfloat16)
+    part = fb[...].astype(jnp.float32).T.astype(jnp.bfloat16)
+    for i in range(2):
+        own_share[pl.ds(SRC * KB, CH // 2), pl.ds(i * 128, 128)] = part[i * 16 : i * 16 + 16]
 
     cut = ROWS // 32 * 16
     me = y * 4 + x
@@ -285,7 +296,7 @@
     own_m.wait()
     for c in exchanged:
         c.wait_recv()
-    for c in stage_1 + stage_2 + [stage_z, across] + shares + exchanged + started:
+    for c in stage_1 + stage_2 + [across] + flags + shares + exchanged + started:
         c.wait_send()
 
 
@@ -304,12 +315,11 @@
             pltpu.VMEM((2, SRC, 4, 2, SEG, BINS), bf),
             pltpu.VMEM((2, 4, SRC, 2, SEG, BINS), bf),
             pltpu.VMEM((2, SRC, 2, SEG, BINS), bf),
-            pltpu.VMEM((2, SRC, 2, SEG, BINS), bf),
-            pltpu.VMEM((1 + SRC, 2, SEG, BINS), bf),
-            pltpu.VMEM((1 + SRC, 2, NTM * SEG, KB), bf),
+            pltpu.VMEM((NTM * SEG, KB), bf),
+            pltpu.VMEM((2, SRC, 2, NTM * SEG, KB), bf),
             pltpu.VMEM((ROWS, 256), bf),
-            pltpu.SemaphoreType.DMA((81,)),
-            pltpu.SemaphoreType.DMA((81,)),
+            pltpu.SemaphoreType.DMA((97,)),
+            pltpu.SemaphoreType.DMA((97,)),
             pltpu.SemaphoreType.DMA((9,)),
         ],
         compiler_params=pltpu.CompilerParams(
@@ -337,7 +347,10 @@
     lax.fori_loop(0, CH, widen, 0)
 
     def flags(block):
-        return g_ref[lax.rem(block, 2), block // 2, pl.ds(SRC * KB, CH), pl.ds(0, 128)]
+        rows = pl.ds(SRC * KB, CH // 2)
+        return jnp.concatenate(
+            [g_ref[lax.rem(block, 2), block // 2, rows, pl.ds(i * 128, 128)] for i in range(2)]
+        )
 
     fr = flags(lax.axis_index("chan"))
     fr = jnp.concatenate([fr, fr], axis=0)
@@ -471,18 +484,16 @@
 
 
 def make_seeds():
-    tau = lax.broadcasted_iota(jnp.int32, (1, BINS), 1)
+    tau = np.arange(BINS)
 
     def pair(freq):
-        angle = ((freq * tau) % (2 * BINS)).astype(jnp.float32) * (math.pi / BINS)
-        return jnp.cos(angle), jnp.sin(angle)
-
-    c1, s1 = pair(lax.broadcasted_iota(jnp.int32, (BINS // 32, 1), 0) * 32)
-    row = lax.broadcasted_iota(jnp.int32, (32, 1), 0)
-    c2, s2 = (
-        (v / math.sqrt(BINS)).reshape(2, 16, BINS) for v in pair(row % 16 * 2 + row // 16)
-    )
-    return c1, s1, c2, s2
+        angle = (np.multiply.outer(freq, tau) % (2 * BINS)) * (math.pi / BINS)
+        return np.cos(angle), np.sin(angle)
+
+    c1, s1 = pair(np.arange(BINS // 32) * 32)
+    c2, s2 = pair(np.add.outer(np.arange(2), 2 * np.arange(16)))
+    scale = 1.0 / math.sqrt(BINS)
+    return [jnp.asarray(v, jnp.float32) for v in (c1, s1, c2 * scale, s2 * scale)]
 
 
 def lags_body(v_ref, c_ref, th_ref, tl_ref, out_ref, xh, xl):

time: 197 us -> 187 us (0.949); the launches traced: 193 us -> 186 us
  Pallas kernels: 185 us -> 181 us
  other arithmetic: 7.52 us -> 4.9 us
    pallas_call x1, Pallas kernels: 105 us -> 102 us  [front(): pl.pallas_call(front_body, out_shape=(jax.ShapeDtypeStruct((CH, 2, NTM *...]
where the time goes in v4:
time: 187 us; the launch traced here: 186 us
  Pallas kernels  181 us (97%)
  other arithmetic  4.9 us (3%)
    pallas_call x1, Pallas kernels, front(): pl.pallas_call(front_body, out_shape=(jax.ShapeDtypeStruct((CH, 2, NTM *...  102 us
    pallas_call x1, Pallas kernels, collect(): pl.pallas_call(collect_body, out_shape=(jax.ShapeDtypeStruct(x.shape, x.d...  42 us
    pallas_call x1, Pallas kernels, correlate(): pl.pallas_call(correlate_body, out_shape=(jax.ShapeDtypeStruct((SRC * CH,...  25.8 us
    pallas_call x1, Pallas kernels, lags(): pl.pallas_call(lags_body, grid=(BINS // step,), out_shape=jax.ShapeDtypeS...  11.4 us

profile of v4, /device:TPU:225, one launch (start us, length us, event | category | flops | bytes accessed | tf_op | source)
XLA Modules:
  0.0 186.4 jit_solution(12371323819407856210)
XLA Ops:
  0.0 0.7 convert_bitcast_fusion
  0.7 0.7 convert_element_type.5
  1.4 0.1 copy.8
  1.5 2.0 %fusion = bf16[32,2,16,1024]{3,2,1,0:T(8,128)(2,1)S(1)} fusion(bf16[32,16,2,1024]{3,2,1,0:T(2,128)(2,1)} %param.7, bf16[32,16]{1,0:T(8,128)(2,1)S(1)} %copy.8), kind=kLoop, calls=%fused_computation.2 | loop fusion | flops 1048576 | bytes 4195328 | tf_op jit(solution)/shard_map/transpose | solution.py:562
  3.5 1.5 pad_maximum_fusion.m
  5.0 102.2 %shard_map.73 = (bf16[32,2,128,128]{3,2,1,0:T(8,128)(2,1)}, bf16[2,16,400,256]{3,2,1,0:T(8,128)(2,1)}) custom-call(s32[3]{0:T(128)} %plan.3, bf16[33,2,16,1024]{3,2,1,0:T(8,128)(2,1)} %pad_maximum_fusion.m), custom_call_target="tpu_custom_call" | custom-call | tf_op jit(solution)/shard_map/pallas_call | solution.py:305
  107.2 25.8 %shard_map.74 = (s16[96,64,128]{2,1,0:T(8,128)(2,1)}, f32[8,16,128]{2,1,0:T(8,128)}) custom-call(s32[3]{0:T(128)} %plan.3, bf16[2,16,400,256]{3,2,1,0:T(8,128)(2,1)} %get-tuple-element.13.g_ref, bf16[32,2,128,128]{3,2,1,0:T(8,128)(2,1)} %get-tuple-element.14.y_ref), custom_call_target="tpu_custom_call" | custom-call | tf_op jit(solution)/shard_map/pallas_call | solution.py:397
  133.1 42.0 %shard_map.75 = (s16[8,768,128]{2,1,0:T(8,128)(2,1)}, f32[8,16,128]{2,1,0:T(8,128)}, bf16[2,2,32,16,1024]{4,3,2,1,0:T(8,128)(2,1)}, bf16[2,2,32,16,1024]{4,3,2,1,0:T(8,128)(2,1)}) custom-call(s16[8,768,128]{2,1,0:T(8,128)(2,1)} %bitcast.16, f32[8,16,128]{2,1,0:T(8,128)} %get-tuple-element.16.c_ref, f32[32,1024]{1,0:T(8,128)} %constant.11.clone.c1, ...), custom_call_target="tpu_custom_call" | custom-call | tf_op jit(solution)/shard_map/pallas_call | solution.py:463
  175.1 11.4 %shard_map.76 = f32[384,2048]{1,0:T(8,128)} custom-call(s16[8,12,2,32,128]{4,3,2,1,0:T(8,128)(2,1)} %bitcast.15, f32[8,16,128]{2,1,0:T(8,128)} %get-tuple-element.18.c_ref, bf16[2,1024,1024]{2,1,0:T(8,128)(2,1)} %bitcast.13, bf16[2,1024,1024]{2,1,0:T(8,128)(2,1)} %bitcast.14), custom_call_target="tpu_custom_call" | custom-call | tf_op jit(solution)/shard_map/pallas_call | solution.py:541
  (4 shorter events, 0.0 us)

commit v5 on v4

--- a/solution.py
+++ b/solution.py
@@ -19,6 +19,7 @@
 BINS = 1024
 KB = BINS // NTM
 ROWS = SRC * KB + CH // 2
+HALF = 48
 EARLY = 16
 TOP = 32766.0
 BIG = 56 * 1024 * 1024
@@ -52,7 +53,12 @@
     return copy
 
 
-def front_body(plan, m, y_out, o_ref, r1, s1, r2, s2, fb, yb, own_share, send, recv, local):
+def stack_body(
+    plan, m, c1, n1, c2, n2, v_ref, d_ref, inv_ref, th_ref, tl_ref,
+    r1, s1, r2, s2, fb, yb, own_share, y_out, o_ref, sa, sq, ra, rq, ob, inv, codes, scales, th, tl,
+    send, recv, local, code_send, code_recv, code_local,
+):
+    f32, bf = jnp.float32, jnp.bfloat16
     y, x, zh, tm = place()
     tms = [lax.rem(tm + d, NTM) for d in range(1, NTM)]
     greet(
@@ -129,6 +135,27 @@
         m.at[pl.ds(0, CH), :, :, my_lanes], y_out.at[:, :, my_rows, :], local.at[1]
     )
     own_m.start()
+
+    def make(e1, carry):
+        cos1 = jnp.broadcast_to(c1[pl.ds(e1, 1), :], (16, BINS))
+        sin1 = jnp.broadcast_to(n1[pl.ds(e1, 1), :], (16, BINS))
+        for parity in range(2):
+            cos = cos1 * c2[parity] - sin1 * n2[parity]
+            sin = -(sin1 * c2[parity] + cos1 * n2[parity])
+            for p, value in enumerate((cos, sin)):
+                high = value.astype(bf)
+                th[parity, p, e1] = high
+                tl[parity, p, e1] = (value - high.astype(f32)).astype(bf)
+        return carry
+
+    lax.fori_loop(0, BINS // 32, make, 0)
+    tables = [
+        pltpu.make_async_copy(th, th_ref, local.at[9]),
+        pltpu.make_async_copy(tl, tl_ref, local.at[10]),
+    ]
+    for c in tables:
+        c.start()
+    scales[...] = jnp.zeros_like(scales)
 
     for c in own_1:
         c.wait()
@@ -274,6 +301,82 @@
             self.passed[r] = (f1, f2)
 
     mine, other = Half(zh), Half(1 - zh)
+
+    def landed(r):
+        for h in (mine, other):
+            for f in h.passed[r]:
+                f.wait_recv()
+
+    def group(g, between):
+        def coords(q):
+            blk, h, ri = q // 4, lax.rem(q // 2, 2), lax.rem(q, 2)
+            return blk, h, up(x + h * (y - x), 3 * ri if g == 0 else 1 + ri)
+
+        def widen(q, carry):
+            blk, h, a = coords(q)
+            for bb in range(4):
+                rows = pl.ds(pl.multiple_of((q * 4 + bb) * KB, KB), KB)
+                slot = bb * (4 - 3 * h) + a * (1 + 3 * h)
+                tile = pl.ds(pl.multiple_of(blk * KB, KB), KB)
+                for p, part in enumerate((sa, sq)):
+                    part[rows, :] = o_ref[h, slot, tile, pl.ds(p * 128, 128)].astype(f32)
+            return carry
+
+        lax.fori_loop(0, 12, widen, 0)
+        between()
+
+        def one(k, to):
+            sources, channels = pl.ds(k, HALF, stride=KB), pl.ds(k, CH, stride=KB)
+            s = jnp.concatenate([sa[sources, :], sq[sources, :]], axis=1).astype(bf)
+            a, q = ra[channels, :], rq[channels, :]
+            real, imag = jnp.concatenate([a, q], axis=1), jnp.concatenate([q, -a], axis=1)
+            both = jnp.concatenate([real, imag], axis=0).astype(bf)
+            res = lax.dot_general(s, both, (((1,), (1,)), ((), ())), preferred_element_type=f32)
+            ob[pl.ds(to, HALF, stride=KB), :] = jnp.concatenate([res, jnp.zeros_like(res)], axis=1)
+
+        def some(i, carry):
+            for t in range(8):
+                one(i * 8 + t, i * 4 + t // 2 + t % 2 * (KB // 2))
+            return carry
+
+        lax.fori_loop(0, KB // 8, some, 0)
+
+        def turn(q, carry):
+            blk, h, a = coords(q)
+            u = 8 * blk + 4 * h + a
+            to, at = u // 3, lax.rem(u, 3)
+            for bb in range(4):
+                block = ob[pl.ds(pl.multiple_of((q * 4 + bb) * KB, KB), KB), :]
+                most = jnp.maximum(jnp.max(jnp.abs(block), axis=0, keepdims=True), 1e-30)
+                code = jnp.round(block * (TOP / most)).T[: 2 * CH]
+                codes[u, bb] = code.astype(jnp.int32).astype(jnp.int16)
+                scales[to, pl.ds(at * 4 + bb, 1), :] = most * (1.0 / TOP)
+
+            @pl.when(to != tm)
+            def _():
+                code_to(u, to, at).start()
+
+            @pl.when(to == tm)
+            def _():
+                code_here(u, at).start()
+
+            return carry
+
+        lax.fori_loop(0, 12, turn, 0)
+
+    def code_to(u, to, at):
+        return pltpu.make_async_remote_copy(
+            src_ref=codes.at[u],
+            dst_ref=v_ref.at[tm, at],
+            send_sem=code_send.at[u],
+            recv_sem=code_recv.at[tm, at],
+            device_id=device(y, x, zh, to),
+            device_id_type=MESH,
+        )
+
+    def code_here(u, at):
+        return pltpu.make_async_copy(codes.at[u], v_ref.at[tm, at], code_local.at[at])
+
     mine.start(own_share)
     mine.first()
     across.wait_recv()
@@ -283,33 +386,101 @@
     other.first()
     mine.forward(1)
     other.forward(0)
-    mine.forward(2)
     other.second()
-    mine.forward(3)
-    for r in (1, 2, 3):
-        other.forward(r)
-    for r in range(4):
-        for h in (mine, other):
-            for f in h.passed[r]:
-                f.wait_recv()
-    own.wait()
+    other.forward(1)
     own_m.wait()
     for c in exchanged:
         c.wait_recv()
+
+    def channel(j, carry):
+        rows = pl.ds(pl.multiple_of(j * KB, KB), KB)
+        for p, part in enumerate((ra, rq)):
+            part[rows, :] = y_out[j, p].astype(f32).T
+        return carry
+
+    lax.fori_loop(0, CH, channel, 0)
+    mine.forward(2)
+    other.forward(2)
+    own.wait()
+    landed(0)
+    landed(1)
+
+    def last():
+        mine.forward(3)
+        other.forward(3)
+
+    group(0, last)
+    landed(2)
+    landed(3)
+    group(1, lambda: None)
+
+    scale_out = [
+        remote(
+            scales.at[t],
+            d_ref.at[tm],
+            send.at[97 + d],
+            recv.at[97 + d],
+            device(y, x, zh, t),
+        )
+        for d, t in enumerate(tms)
+    ]
+    own_d = pltpu.make_async_copy(scales.at[tm], d_ref.at[tm], local.at[11])
+    own_d.start()
+
+    def flags_of(block):
+        rows = pl.ds(SRC * KB, CH // 2)
+        return jnp.concatenate(
+            [o_ref[lax.rem(block, 2), block // 2, rows, pl.ds(i * 128, 128)] for i in range(2)]
+        )
+
+    fr = flags_of(lax.axis_index("chan"))
+    fr = jnp.concatenate([fr] * 4, axis=0)
+    for b in range(SRC):
+        count = lax.dot_general(
+            flags_of(plan[b]), fr, (((1,), (1,)), ((), ())), preferred_element_type=f32
+        )
+        inv[pl.ds(b * CH, CH), :] = 1.0 / jnp.maximum(count, 1.0)
+    inv_ref[...] = jnp.zeros_like(inv_ref)
+    for i in range(12):
+        inv_ref[pl.ds(i, 1), :] = inv[pl.ds(tm * 12 + i, 1), :]
+
+    for t in tms:
+        for i in range(3):
+            pltpu.make_async_remote_copy(
+                src_ref=codes.at[i],
+                dst_ref=v_ref.at[t, i],
+                send_sem=code_send.at[i],
+                recv_sem=code_recv.at[t, i],
+                device_id=device(y, x, zh, t),
+                device_id_type=MESH,
+            ).wait_recv()
+            code_to(t * 3 + i, t, i).wait_send()
+    for i in range(3):
+        code_here(tm * 3 + i, i).wait()
+    for c in scale_out:
+        c.wait()
+    own_d.wait()
+    for c in tables:
+        c.wait()
     for c in stage_1 + stage_2 + [across] + flags + shares + exchanged + started:
         c.wait_send()
 
 
-def front(plan, m):
-    bf = jnp.bfloat16
+def stack(plan, m, seeds):
+    bf, f32 = jnp.bfloat16, jnp.float32
+    hbm, vmem = pl.BlockSpec(memory_space=ANY), pl.BlockSpec(memory_space=pltpu.VMEM)
+    table = (2, 2, BINS // 32, 16, BINS)
     return pl.pallas_call(
-        front_body,
+        stack_body,
         out_shape=(
-            jax.ShapeDtypeStruct((CH, 2, NTM * SEG, KB), bf),
-            jax.ShapeDtypeStruct((2, 16, ROWS, 256), bf),
+            jax.ShapeDtypeStruct((NTM, 3, 4, 2 * CH, KB), jnp.int16),
+            jax.ShapeDtypeStruct((NTM, 16, KB), f32),
+            jax.ShapeDtypeStruct((16, 128), f32),
+            jax.ShapeDtypeStruct(table, bf),
+            jax.ShapeDtypeStruct(table, bf),
         ),
-        in_specs=[pl.BlockSpec(memory_space=pltpu.SMEM), pl.BlockSpec(memory_space=ANY)],
-        out_specs=(pl.BlockSpec(memory_space=ANY), pl.BlockSpec(memory_space=ANY)),
+        in_specs=[pl.BlockSpec(memory_space=pltpu.SMEM), hbm, vmem, vmem, vmem, vmem],
+        out_specs=(hbm, hbm, vmem, hbm, hbm),
         scratch_shapes=[
             pltpu.VMEM((2, 4, 4, 2, SEG, BINS), bf),
             pltpu.VMEM((2, SRC, 4, 2, SEG, BINS), bf),
@@ -318,169 +489,29 @@
             pltpu.VMEM((NTM * SEG, KB), bf),
             pltpu.VMEM((2, SRC, 2, NTM * SEG, KB), bf),
             pltpu.VMEM((ROWS, 256), bf),
-            pltpu.SemaphoreType.DMA((97,)),
-            pltpu.SemaphoreType.DMA((97,)),
-            pltpu.SemaphoreType.DMA((9,)),
+            pltpu.VMEM((CH, 2, NTM * SEG, KB), bf),
+            pltpu.VMEM((2, 16, ROWS, 256), bf),
+            pltpu.VMEM((HALF * KB, 128), f32),
+            pltpu.VMEM((HALF * KB, 128), f32),
+            pltpu.VMEM((CH * KB, 128), f32),
+            pltpu.VMEM((CH * KB, 128), f32),
+            pltpu.VMEM((HALF * KB, 128), f32),
+            pltpu.VMEM((SRC * CH, 128), f32),
+            pltpu.VMEM((24, 4, 2 * CH, KB), jnp.int16),
+            pltpu.VMEM((NTM, 16, KB), f32),
+            pltpu.VMEM(table, bf),
+            pltpu.VMEM(table, bf),
+            pltpu.SemaphoreType.DMA((104,)),
+            pltpu.SemaphoreType.DMA((104,)),
+            pltpu.SemaphoreType.DMA((12,)),
+            pltpu.SemaphoreType.DMA((24,)),
+            pltpu.SemaphoreType.DMA((NTM, 3)),
+            pltpu.SemaphoreType.DMA((3,)),
         ],
         compiler_params=pltpu.CompilerParams(
             collective_id=0, has_side_effects=True, vmem_limit_bytes=BIG
         ),
-    )(plan, m)
-
-
-def correlate_body(plan, g_ref, y_ref, out_ref, scale_ref, sa, sq, ra, rq, ob):
-    f32, bf = jnp.float32, jnp.bfloat16
-
-    def widen(j, carry):
-        zh, a, c = j // 16, lax.rem(j // 4, 4), lax.rem(j, 4)
-        slot = c * (4 - 3 * zh) + a * (1 + 3 * zh)
-        for b in range(SRC):
-            rows = pl.ds(pl.multiple_of((b * CH + j) * KB, KB), KB)
-            for p, part in enumerate((sa, sq)):
-                lanes = pl.ds(p * 128, 128)
-                part[rows, :] = g_ref[zh, slot, pl.ds(b * KB, KB), lanes].astype(f32)
-        rows = pl.ds(pl.multiple_of(j * KB, KB), KB)
-        for p, part in enumerate((ra, rq)):
-            part[rows, :] = y_ref[j, p].astype(f32).T
-        return carry
-
-    lax.fori_loop(0, CH, widen, 0)
-
-    def flags(block):
-        rows = pl.ds(SRC * KB, CH // 2)
-        return jnp.concatenate(
-            [g_ref[lax.rem(block, 2), block // 2, rows, pl.ds(i * 128, 128)] for i in range(2)]
-        )
-
-    fr = flags(lax.axis_index("chan"))
-    fr = jnp.concatenate([fr, fr], axis=0)
-    counts = []
-    for b in range(SRC):
-        fs = flags(plan[b])
-        counts.append(
-            lax.dot_general(fs, fr, (((1,), (1,)), ((), ())), preferred_element_type=f32)
-        )
-    inverse = 1.0 / jnp.maximum(jnp.concatenate(counts, axis=0), 1.0)
-
-    def one(k, to):
-        sources, channels = pl.ds(k, SRC * CH, stride=KB), pl.ds(k, CH, stride=KB)
-        s = jnp.concatenate([sa[sources, :], sq[sources, :]], axis=1).astype(bf)
-        a, q = ra[channels, :], rq[channels, :]
-        real, imag = jnp.concatenate([a, q], axis=1), jnp.concatenate([q, -a], axis=1)
-        both = jnp.concatenate([real, imag], axis=0).astype(bf)
-        res = lax.dot_general(s, both, (((1,), (1,)), ((), ())), preferred_element_type=f32)
-        res = res * inverse
-        ob[pl.ds(to, SRC * CH, stride=KB), :] = jnp.concatenate([res, jnp.zeros_like(res)], axis=1)
-
-    def some(i, carry):
-        for u in range(8):
-            one(i * 8 + u, i * 4 + u // 2 + u % 2 * (KB // 2))
-        return carry
-
-    lax.fori_loop(0, KB // 8, some, 0)
-
-    def turn(t, carry):
-        for i in range(12):
-            s = t * 12 + i
-            block = ob[pl.ds(pl.multiple_of(s * KB, KB), KB), pl.ds(0, 2 * CH)].T
-            most = jnp.maximum(jnp.max(jnp.abs(block), axis=0, keepdims=True), 1e-30)
-            code = jnp.round(block * (TOP / most)).astype(jnp.int32)
-            out_ref[s] = code.astype(jnp.int16)
-            scale_ref[t, pl.ds(i, 1), :] = most * (1.0 / TOP)
-        return carry
-
-    lax.fori_loop(0, NTM, turn, 0)
-
-
-def correlate(plan, g, y):
-    vmem = pl.BlockSpec(memory_space=pltpu.VMEM)
-    return pl.pallas_call(
-        correlate_body,
-        out_shape=(
-            jax.ShapeDtypeStruct((SRC * CH, 2 * CH, KB), jnp.int16),
-            jax.ShapeDtypeStruct((NTM, 16, KB), jnp.float32),
-        ),
-        in_specs=[pl.BlockSpec(memory_space=pltpu.SMEM), vmem, vmem],
-        out_specs=(vmem, vmem),
-        scratch_shapes=[
-            pltpu.VMEM((SRC * CH * KB, 128), jnp.float32),
-            pltpu.VMEM((SRC * CH * KB, 128), jnp.float32),
-            pltpu.VMEM((CH * KB, 128), jnp.float32),
-            pltpu.VMEM((CH * KB, 128), jnp.float32),
-            pltpu.VMEM((SRC * CH * KB, 128), jnp.float32),
-        ],
-        compiler_params=pltpu.CompilerParams(vmem_limit_bytes=BIG),
-    )(plan, g, y)
-
-
-def collect_body(
-    x_ref, c_ref, c1, s1, c2, s2, v_ref, d_ref, th_ref, tl_ref, th, tl, send, recv, local
-):
-    y, x, zh, tm = place()
-    tms = [lax.rem(tm + d, NTM) for d in range(1, NTM)]
-    greet([device(y, x, zh, t) for t in tms])
-    copies = []
-    for d in range(1, NTM):
-        t = tms[d - 1]
-        for i, (src, dst) in enumerate(((x_ref, v_ref), (c_ref, d_ref))):
-            copies.append(
-                remote(src.at[t], dst.at[tm], send.at[i, d], recv.at[i, d], device(y, x, zh, t))
-            )
-    own = [
-        pltpu.make_async_copy(src.at[tm], dst.at[tm], local.at[i])
-        for i, (src, dst) in enumerate(((x_ref, v_ref), (c_ref, d_ref)))
-    ]
-    for c in own:
-        c.start()
-
-    def make(e1, carry):
-        cos1 = jnp.broadcast_to(c1[pl.ds(e1, 1), :], (16, BINS))
-        sin1 = jnp.broadcast_to(s1[pl.ds(e1, 1), :], (16, BINS))
-        for parity in range(2):
-            cos = cos1 * c2[parity] - sin1 * s2[parity]
-            sin = -(sin1 * c2[parity] + cos1 * s2[parity])
-            for p, value in enumerate((cos, sin)):
-                high = value.astype(jnp.bfloat16)
-                low = (value - high.astype(jnp.float32)).astype(jnp.bfloat16)
-                th[parity, p, e1] = high
-                tl[parity, p, e1] = low
-        return carry
-
-    lax.fori_loop(0, BINS // 32, make, 0)
-    out = [
-        pltpu.make_async_copy(th, th_ref, local.at[2]),
-        pltpu.make_async_copy(tl, tl_ref, local.at[3]),
-    ]
-    for c in out:
-        c.start()
-    for c in own + copies + out:
-        c.wait()
-
-
-def collect(x, c, seeds):
-    hbm, vmem = pl.BlockSpec(memory_space=ANY), pl.BlockSpec(memory_space=pltpu.VMEM)
-    table = (2, 2, BINS // 32, 16, BINS)
-    return pl.pallas_call(
-        collect_body,
-        out_shape=(
-            jax.ShapeDtypeStruct(x.shape, x.dtype),
-            jax.ShapeDtypeStruct(c.shape, c.dtype),
-            jax.ShapeDtypeStruct(table, jnp.bfloat16),
-            jax.ShapeDtypeStruct(table, jnp.bfloat16),
-        ),
-        in_specs=[hbm, hbm, vmem, vmem, vmem, vmem],
-        out_specs=(hbm, hbm, hbm, hbm),
-        scratch_shapes=[
-            pltpu.VMEM(table, jnp.bfloat16),
-            pltpu.VMEM(table, jnp.bfloat16),
-            pltpu.SemaphoreType.DMA((2, NTM)),
-            pltpu.SemaphoreType.DMA((2, NTM)),
-            pltpu.SemaphoreType.DMA((4,)),
-        ],
-        compiler_params=pltpu.CompilerParams(
-            collective_id=2, has_side_effects=True, vmem_limit_bytes=BIG
-        ),
-    )(x, c, *seeds)
+    )(plan, m, *seeds)
 
 
 def make_seeds():
@@ -496,20 +527,22 @@
     return [jnp.asarray(v, jnp.float32) for v in (c1, s1, c2 * scale, s2 * scale)]
 
 
-def lags_body(v_ref, c_ref, th_ref, tl_ref, out_ref, xh, xl):
+def lags_body(v_ref, c_ref, inv_ref, th_ref, tl_ref, out_ref, xh, xl, factor):
     step = th_ref.shape[2]
 
     @pl.when(pl.program_id(0) == 0)
     def _():
         lane = lax.broadcasted_iota(jnp.int32, (CH, KB), 1)
-
-        def split(s, carry):
-            rows = pl.ds(pl.multiple_of(s * CH, CH), CH)
+        for j in range(NTM):
+            factor[j] = (c_ref[j] * inv_ref[...]).T
+
+        for s in range(12):
+            rows = pl.ds(s * CH, CH)
             for p in range(2):
                 for j in range(NTM // 2):
                     a, b = (
                         v_ref[2 * j + i, s, p].astype(jnp.int32).astype(jnp.float32)
-                        * c_ref[2 * j + i, pl.ds(s, 1), :]
+                        * factor[2 * j + i, pl.ds(p * CH, CH), s : s + 1]
                         for i in range(2)
                     )
                     even = jnp.where(lane < KB // 2, a, pltpu.roll(b, KB // 2, 1))
@@ -521,9 +554,6 @@
                         xl[parity, rows, lanes] = (value - high.astype(jnp.float32)).astype(
                             jnp.bfloat16
                         )
-            return carry
-
-        lax.fori_loop(0, 12, split, 0)
 
     def dot(a, b):
         return jnp.dot(a, b, preferred_element_type=jnp.float32)
@@ -536,7 +566,7 @@
     out_ref[:, pl.ds(pl.multiple_of(at + BINS, step), step)] = even + odd
 
 
-def lags(v, c, th, tl):
+def lags(v, c, inv, th, tl):
     rows, step = 12 * CH, 256
     return pl.pallas_call(
         lags_body,
@@ -545,6 +575,7 @@
         in_specs=[
             pl.BlockSpec((NTM, 12, 2, CH, KB), lambda g: (0, 0, 0, 0, 0)),
             pl.BlockSpec((NTM, 16, KB), lambda g: (0, 0, 0)),
+            pl.BlockSpec((16, 128), lambda g: (0, 0)),
             pl.BlockSpec((2, BINS, step), lambda g: (0, 0, g)),
             pl.BlockSpec((2, BINS, step), lambda g: (0, 0, g)),
         ],
@@ -552,9 +583,10 @@
         scratch_shapes=[
             pltpu.VMEM((2, rows, BINS), jnp.bfloat16),
             pltpu.VMEM((2, rows, BINS), jnp.bfloat16),
+            pltpu.VMEM((NTM, 128, 16), jnp.float32),
         ],
         compiler_params=pltpu.CompilerParams(vmem_limit_bytes=BIG),
-    )(v, c, th, tl)
+    )(v, c, inv, th, tl)
 
 
 def shards(spectra, quality, plan):
@@ -562,11 +594,9 @@
     masked = (spectra * flags[:, :, None, None]).transpose(0, 2, 1, 3)
     row = jnp.tile(jnp.pad(flags.T, ((0, 0), (0, KB - CH))), (1, NTM))
     m = jnp.concatenate([masked, jnp.broadcast_to(row, (1, 2, SEG, BINS))], axis=0)
-    y, g = front(plan, m)
-    x, c = correlate(plan, g, y)
-    v, c, th, tl = collect(x.reshape(NTM, 12 * 2 * CH, KB), c, make_seeds())
+    v, c, inv, th, tl = stack(plan, m, make_seeds())
     th, tl = (t.reshape(2, BINS, BINS) for t in (th, tl))
-    out = lags(v.reshape(NTM, 12, 2, CH, KB), c, th, tl)
+    out = lags(v.reshape(NTM, 12, 2, CH, KB), c, inv, th, tl)
     return out.reshape(12, CH, 2 * BINS)
 
 

time: 187 us -> 165 us (0.88); the launches traced: 186 us -> 162 us
  Pallas kernels: 181 us -> 157 us
    pallas_call x3 -> x1, Pallas kernels: 170 us -> 140 us  [stack(): pl.pallas_call(stack_body, out_shape=(jax.ShapeDtypeStruct((NTM, 3, 4, 2...]
    pallas_call x1, Pallas kernels: 11.4 us -> 17.5 us  [lags(): pl.pallas_call(lags_body, grid=(BINS // step,), out_shape=jax.ShapeDtypeS...]
where the time goes in v5:
time: 165 us; the launch traced here: 162 us
  Pallas kernels  157 us (95%)
  other arithmetic  4.9 us (3%)
    pallas_call x1, Pallas kernels, stack(): pl.pallas_call(stack_body, out_shape=(jax.ShapeDtypeStruct((NTM, 3, 4, 2...  140 us
    pallas_call x1, Pallas kernels, lags(): pl.pallas_call(lags_body, grid=(BINS // step,), out_shape=jax.ShapeDtypeS...  17.5 us

profile of v5, /device:TPU:225, one launch (start us, length us, event | category | flops | bytes accessed | tf_op | source)
XLA Modules:
  0.0 162.2 jit_solution(16501793301874239975)
XLA Ops:
  0.0 0.7 convert_bitcast_fusion
  0.7 0.7 convert_element_type.5
  1.4 0.1 copy.8
  1.5 2.0 %fusion = bf16[32,2,16,1024]{3,2,1,0:T(8,128)(2,1)S(1)} fusion(bf16[32,16,2,1024]{3,2,1,0:T(2,128)(2,1)} %param.7, bf16[32,16]{1,0:T(8,128)(2,1)S(1)} %copy.8), kind=kLoop, calls=%fused_computation.2 | loop fusion | flops 1048576 | bytes 4195328 | tf_op jit(solution)/shard_map/transpose | solution.py:594
  3.5 1.5 pad_maximum_fusion.m
  5.0 139.6 %shard_map.73 = (s16[8,3,4,64,128]{4,3,2,1,0:T(8,128)(2,1)}, f32[8,16,128]{2,1,0:T(8,128)}, f32[16,128]{1,0:T(8,128)}, bf16[2,2,32,16,1024]{4,3,2,1,0:T(8,128)(2,1)}, bf16[2,2,32,16,1024]{4,3,2,1,0:T(8,128)(2,1)}) custom-call(s32[3]{0:T(128)} %plan.1, bf16[33,2,16,1024]{3,2,1,0:T(8,128)(2,1)} %pad_maximum_fusion.m, f32[32,1024]{1,0:T(8,128)} %constant.11.clone.c1, ...), custom_call_target="tpu_custom_call" | custom-call | tf_op jit(solution)/shard_map/pallas_call | solution.py:473
  144.7 17.5 %shard_map.74 = f32[384,2048]{1,0:T(8,128)} custom-call(s16[8,12,2,32,128]{4,3,2,1,0:T(8,128)(2,1)} %bitcast.14, f32[8,16,128]{2,1,0:T(8,128)} %get-tuple-element.11.c_ref, f32[16,128]{1,0:T(8,128)} %get-tuple-element.12.inv_ref, bf16[2,1024,1024]{2,1,0:T(8,128)(2,1)} %bitcast.12, bf16[2,1024,1024]{2,1,0:T(8,128)(2,1)} %bitcast.13), custom_call_target="tpu_custom_call" | custom-call | tf_op jit(solution)/shard_map/pallas_call | solution.py:571
  (4 shorter events, 0.0 us)

commit v6 on v5

--- a/solution.py
+++ b/solution.py
@@ -54,7 +54,7 @@
 
 
 def stack_body(
-    plan, m, c1, n1, c2, n2, v_ref, d_ref, inv_ref, th_ref, tl_ref,
+    plan, m, fl, c1, n1, c2, n2, v_ref, d_ref, inv_ref, th_ref, tl_ref,
     r1, s1, r2, s2, fb, yb, own_share, y_out, o_ref, sa, sq, ra, rq, ob, inv, codes, scales, th, tl,
     send, recv, local, code_send, code_recv, code_local,
 ):
@@ -120,7 +120,7 @@
         c.start()
     flags = [
         remote(
-            m.at[CH, 0, :, bins_of(t)],
+            fl,
             fb.at[my_rows, :],
             send.at[24 + d],
             recv.at[24 + d],
@@ -128,11 +128,11 @@
         )
         for d, t in enumerate(tms, 1)
     ]
-    own_f = pltpu.make_async_copy(m.at[CH, 0, :, my_lanes], fb.at[my_rows, :], local.at[5])
+    own_f = pltpu.make_async_copy(fl, fb.at[my_rows, :], local.at[5])
     own_f.start()
     exchanged = main(0, EARLY, 73)
     own_m = pltpu.make_async_copy(
-        m.at[pl.ds(0, CH), :, :, my_lanes], y_out.at[:, :, my_rows, :], local.at[1]
+        m.at[:, :, :, my_lanes], y_out.at[:, :, my_rows, :], local.at[1]
     )
     own_m.start()
 
@@ -216,7 +216,6 @@
         s2.at[zh, :, :, :, my_lanes], yb.at[zh, :, :, my_rows, :], local.at[4]
     )
     own_s.start()
-    exchanged += main(EARLY, CH - EARLY, 15)
     own_s.wait()
     own_f.wait()
     for c in flags + shares:
@@ -307,10 +306,12 @@
             for f in h.passed[r]:
                 f.wait_recv()
 
-    def group(g, between):
+    def group(count, first, step, between, during):
+        size = 24 * count
+
         def coords(q):
-            blk, h, ri = q // 4, lax.rem(q // 2, 2), lax.rem(q, 2)
-            return blk, h, up(x + h * (y - x), 3 * ri if g == 0 else 1 + ri)
+            blk, h, ri = q // (2 * count), lax.rem(q // count, 2), lax.rem(q, count)
+            return blk, h, up(x + h * (y - x), first + step * ri)
 
         def widen(q, carry):
             blk, h, a = coords(q)
@@ -322,24 +323,26 @@
                     part[rows, :] = o_ref[h, slot, tile, pl.ds(p * 128, 128)].astype(f32)
             return carry
 
-        lax.fori_loop(0, 12, widen, 0)
+        lax.fori_loop(0, 6 * count, widen, 0)
         between()
 
         def one(k, to):
-            sources, channels = pl.ds(k, HALF, stride=KB), pl.ds(k, CH, stride=KB)
+            sources, channels = pl.ds(k, size, stride=KB), pl.ds(k, CH, stride=KB)
             s = jnp.concatenate([sa[sources, :], sq[sources, :]], axis=1).astype(bf)
             a, q = ra[channels, :], rq[channels, :]
             real, imag = jnp.concatenate([a, q], axis=1), jnp.concatenate([q, -a], axis=1)
             both = jnp.concatenate([real, imag], axis=0).astype(bf)
             res = lax.dot_general(s, both, (((1,), (1,)), ((), ())), preferred_element_type=f32)
-            ob[pl.ds(to, HALF, stride=KB), :] = jnp.concatenate([res, jnp.zeros_like(res)], axis=1)
+            ob[pl.ds(to, size, stride=KB), :] = jnp.concatenate([res, jnp.zeros_like(res)], axis=1)
 
         def some(i, carry):
             for t in range(8):
                 one(i * 8 + t, i * 4 + t // 2 + t % 2 * (KB // 2))
             return carry
 
-        lax.fori_loop(0, KB // 8, some, 0)
+        lax.fori_loop(0, KB // 16, some, 0)
+        during()
+        lax.fori_loop(KB // 16, KB // 8, some, 0)
 
         def turn(q, carry):
             blk, h, a = coords(q)
@@ -362,7 +365,7 @@
 
             return carry
 
-        lax.fori_loop(0, 12, turn, 0)
+        lax.fori_loop(0, 6 * count, turn, 0)
 
     def code_to(u, to, at):
         return pltpu.make_async_remote_copy(
@@ -378,6 +381,7 @@
         return pltpu.make_async_copy(codes.at[u], v_ref.at[tm, at], code_local.at[at])
 
     mine.start(own_share)
+    exchanged += main(EARLY, CH - EARLY, 15)
     mine.first()
     across.wait_recv()
     other.start()
@@ -400,19 +404,14 @@
 
     lax.fori_loop(0, CH, channel, 0)
     mine.forward(2)
-    other.forward(2)
     own.wait()
     landed(0)
+    group(1, 0, 0, lambda: other.forward(2), lambda: mine.forward(3))
     landed(1)
-
-    def last():
-        mine.forward(3)
-        other.forward(3)
-
-    group(0, last)
     landed(2)
+    group(2, 3, -2, lambda: other.forward(3), lambda: None)
     landed(3)
-    group(1, lambda: None)
+    group(1, 2, 0, lambda: None, lambda: None)
 
     scale_out = [
         remote(
@@ -466,7 +465,7 @@
         c.wait_send()
 
 
-def stack(plan, m, seeds):
+def stack(plan, m, fl, seeds):
     bf, f32 = jnp.bfloat16, jnp.float32
     hbm, vmem = pl.BlockSpec(memory_space=ANY), pl.BlockSpec(memory_space=pltpu.VMEM)
     table = (2, 2, BINS // 32, 16, BINS)
@@ -479,7 +478,7 @@
             jax.ShapeDtypeStruct(table, bf),
             jax.ShapeDtypeStruct(table, bf),
         ),
-        in_specs=[pl.BlockSpec(memory_space=pltpu.SMEM), hbm, vmem, vmem, vmem, vmem],
+        in_specs=[pl.BlockSpec(memory_space=pltpu.SMEM), hbm, vmem, vmem, vmem, vmem, vmem],
         out_specs=(hbm, hbm, vmem, hbm, hbm),
         scratch_shapes=[
             pltpu.VMEM((2, 4, 4, 2, SEG, BINS), bf),
@@ -511,7 +510,7 @@
         compiler_params=pltpu.CompilerParams(
             collective_id=0, has_side_effects=True, vmem_limit_bytes=BIG
         ),
-    )(plan, m, *seeds)
+    )(plan, m, fl, *seeds)
 
 
 def make_seeds():
@@ -536,24 +535,28 @@
         for j in range(NTM):
             factor[j] = (c_ref[j] * inv_ref[...]).T
 
-        for s in range(12):
-            rows = pl.ds(s * CH, CH)
-            for p in range(2):
-                for j in range(NTM // 2):
-                    a, b = (
-                        v_ref[2 * j + i, s, p].astype(jnp.int32).astype(jnp.float32)
-                        * factor[2 * j + i, pl.ds(p * CH, CH), s : s + 1]
-                        for i in range(2)
+        def split(q, carry):
+            p, j = q // 4, lax.rem(q, 4)
+            lanes = pl.ds(pl.multiple_of(q * KB, KB), KB)
+            part = pl.ds(pl.multiple_of(p * CH, CH), CH)
+            for s in range(12):
+                rows = pl.ds(s * CH, CH)
+                a, b = (
+                    v_ref[2 * j + i, s, p].astype(jnp.int32).astype(jnp.float32)
+                    * factor[2 * j + i, part, s : s + 1]
+                    for i in range(2)
+                )
+                even = jnp.where(lane < KB // 2, a, pltpu.roll(b, KB // 2, 1))
+                odd = jnp.where(lane < KB // 2, pltpu.roll(a, KB // 2, 1), b)
+                for parity, value in enumerate((even, odd)):
+                    high = value.astype(jnp.bfloat16)
+                    xh[parity, rows, lanes] = high
+                    xl[parity, rows, lanes] = (value - high.astype(jnp.float32)).astype(
+                        jnp.bfloat16
                     )
-                    even = jnp.where(lane < KB // 2, a, pltpu.roll(b, KB // 2, 1))
-                    odd = jnp.where(lane < KB // 2, pltpu.roll(a, KB // 2, 1), b)
-                    lanes = pl.ds(p * (BINS // 2) + j * KB, KB)
-                    for parity, value in enumerate((even, odd)):
-                        high = value.astype(jnp.bfloat16)
-                        xh[parity, rows, lanes] = high
-                        xl[parity, rows, lanes] = (value - high.astype(jnp.float32)).astype(
-                            jnp.bfloat16
-                        )
+            return carry
+
+        lax.fori_loop(0, 2 * NTM // 2, split, 0)
 
     def dot(a, b):
         return jnp.dot(a, b, preferred_element_type=jnp.float32)
@@ -591,10 +594,9 @@
 
 def shards(spectra, quality, plan):
     flags = quality.astype(jnp.bfloat16)
-    masked = (spectra * flags[:, :, None, None]).transpose(0, 2, 1, 3)
-    row = jnp.tile(jnp.pad(flags.T, ((0, 0), (0, KB - CH))), (1, NTM))
-    m = jnp.concatenate([masked, jnp.broadcast_to(row, (1, 2, SEG, BINS))], axis=0)
-    v, c, inv, th, tl = stack(plan, m, make_seeds())
+    m = (spectra * flags[:, :, None, None]).transpose(0, 2, 1, 3)
+    fl = jnp.pad(flags.T, ((0, 0), (0, KB - CH)))
+    v, c, inv, th, tl = stack(plan, m, fl, make_seeds())
     th, tl = (t.reshape(2, BINS, BINS) for t in (th, tl))
     out = lags(v.reshape(NTM, 12, 2, CH, KB), c, inv, th, tl)
     return out.reshape(12, CH, 2 * BINS)

time: 165 us -> 151 us (0.915)
  Pallas kernels: 157 us -> 144 us
    pallas_call x1, Pallas kernels: 140 us -> 129 us  [stack(): pl.pallas_call(stack_body, out_shape=(jax.ShapeDtypeStruct((NTM, 3, 4, 2...]
    pallas_call x1, Pallas kernels: 17.5 us -> 14.9 us  [lags(): pl.pallas_call(lags_body, grid=(BINS // step,), out_shape=jax.ShapeDtypeS...]
where the time goes in v6:
time: 151 us; the launch traced here: 149 us
  Pallas kernels  144 us (95%)
  other arithmetic  4.68 us (3%)
    pallas_call x1, Pallas kernels, stack(): pl.pallas_call(stack_body, out_shape=(jax.ShapeDtypeStruct((NTM, 3, 4, 2...  129 us
    pallas_call x1, Pallas kernels, lags(): pl.pallas_call(lags_body, grid=(BINS // step,), out_shape=jax.ShapeDtypeS...  14.9 us
    transpose x1, other arithmetic, shards(): m = (spectra * flags[:, :, None, None]).transpose(0, 2, 1, 3)  3.29 us

profile of v6, /device:TPU:225, one launch (start us, length us, event | category | flops | bytes accessed | tf_op | source)
XLA Modules:
  0.0 148.9 jit_solution(11599534394725562163)
XLA Ops:
  0.0 0.7 convert_bitcast_fusion
  0.7 0.6 pad.4.fl
  1.3 0.7 convert_element_type.5
  2.0 0.1 copy.8
  2.1 3.3 %fusion.m = bf16[32,2,16,1024]{3,2,1,0:T(8,128)(2,1)} fusion(bf16[32,16,2,1024]{3,2,1,0:T(2,128)(2,1)} %param.7, bf16[32,16]{1,0:T(8,128)(2,1)S(1)} %copy.8), kind=kLoop, calls=%fused_computation.1 | loop fusion | flops 1048576 | bytes 4195328 | tf_op jit(solution)/shard_map/transpose | solution.py:597
  5.4 128.7 %shard_map.73 = (s16[8,3,4,64,128]{4,3,2,1,0:T(8,128)(2,1)}, f32[8,16,128]{2,1,0:T(8,128)}, f32[16,128]{1,0:T(8,128)}, bf16[2,2,32,16,1024]{4,3,2,1,0:T(8,128)(2,1)}, bf16[2,2,32,16,1024]{4,3,2,1,0:T(8,128)(2,1)}) custom-call(s32[3]{0:T(128)} %plan.1, bf16[32,2,16,1024]{3,2,1,0:T(8,128)(2,1)} %fusion.m, bf16[16,128]{1,0:T(8,128)(2,1)} %pad.4.fl, ...), custom_call_target="tpu_custom_call" | custom-call | tf_op jit(solution)/shard_map/pallas_call | solution.py:472
  134.0 14.9 %shard_map.74 = f32[384,2048]{1,0:T(8,128)} custom-call(s16[8,12,2,32,128]{4,3,2,1,0:T(8,128)(2,1)} %bitcast.10, f32[8,16,128]{2,1,0:T(8,128)} %get-tuple-element.11.c_ref, f32[16,128]{1,0:T(8,128)} %get-tuple-element.12.inv_ref, bf16[2,1024,1024]{2,1,0:T(8,128)(2,1)} %bitcast.8, bf16[2,1024,1024]{2,1,0:T(8,128)(2,1)} %bitcast.9), custom_call_target="tpu_custom_call" | custom-call | tf_op jit(solution)/shard_map/pallas_call | solution.py:574

commit v7 on v6

--- a/solution.py
+++ b/solution.py
@@ -55,7 +55,7 @@
 
 def stack_body(
     plan, m, fl, c1, n1, c2, n2, v_ref, d_ref, inv_ref, th_ref, tl_ref,
-    r1, s1, r2, s2, fb, yb, own_share, y_out, o_ref, sa, sq, ra, rq, ob, inv, codes, scales, th, tl,
+    r1, s1, r2, s2, fb, yb, own_share, y_out, o_ref, sa, sq, ra, rq, turned, ob, inv, codes, scales, th, tl,
     send, recv, local, code_send, code_recv, code_local,
 ):
     f32, bf = jnp.float32, jnp.bfloat16
@@ -329,9 +329,13 @@
         def one(k, to):
             sources, channels = pl.ds(k, size, stride=KB), pl.ds(k, CH, stride=KB)
             s = jnp.concatenate([sa[sources, :], sq[sources, :]], axis=1).astype(bf)
-            a, q = ra[channels, :], rq[channels, :]
-            real, imag = jnp.concatenate([a, q], axis=1), jnp.concatenate([q, -a], axis=1)
-            both = jnp.concatenate([real, imag], axis=0).astype(bf)
+            if first == 0:
+                a, q = ra[channels, :], rq[channels, :]
+                real, imag = jnp.concatenate([a, q], axis=1), jnp.concatenate([q, -a], axis=1)
+                both = jnp.concatenate([real, imag], axis=0).astype(bf)
+                turned[k] = both
+            else:
+                both = turned[k]
             res = lax.dot_general(s, both, (((1,), (1,)), ((), ())), preferred_element_type=f32)
             ob[pl.ds(to, size, stride=KB), :] = jnp.concatenate([res, jnp.zeros_like(res)], axis=1)
 
@@ -494,6 +498,7 @@
             pltpu.VMEM((HALF * KB, 128), f32),
             pltpu.VMEM((CH * KB, 128), f32),
             pltpu.VMEM((CH * KB, 128), f32),
+            pltpu.VMEM((KB, 2 * CH, 256), bf),
             pltpu.VMEM((HALF * KB, 128), f32),
             pltpu.VMEM((SRC * CH, 128), f32),
             pltpu.VMEM((24, 4, 2 * CH, KB), jnp.int16),

time: 151 us -> 149 us (0.987)
  Pallas kernels: 144 us -> 142 us
    pallas_call x1, Pallas kernels: 129 us -> 127 us  [stack(): pl.pallas_call(stack_body, out_shape=(jax.ShapeDtypeStruct((NTM, 3, 4, 2...]
where the time goes in v7:
time: 149 us; the launch traced here: 147 us
  Pallas kernels  142 us (95%)
  other arithmetic  4.68 us (3%)
    pallas_call x1, Pallas kernels, stack(): pl.pallas_call(stack_body, out_shape=(jax.ShapeDtypeStruct((NTM, 3, 4, 2...  127 us
    pallas_call x1, Pallas kernels, lags(): pl.pallas_call(lags_body, grid=(BINS // step,), out_shape=jax.ShapeDtypeS...  14.9 us
    transpose x1, other arithmetic, shards(): m = (spectra * flags[:, :, None, None]).transpose(0, 2, 1, 3)  3.29 us

profile of v7, /device:TPU:225, one launch (start us, length us, event | category | flops | bytes accessed | tf_op | source)
XLA Modules:
  0.0 147.0 jit_solution(11250844027184514461)
XLA Ops:
  0.0 0.7 convert_bitcast_fusion
  0.7 0.6 pad.4.fl
  1.3 0.7 convert_element_type.5
  2.0 0.1 copy.8
  2.1 3.3 %fusion.m = bf16[32,2,16,1024]{3,2,1,0:T(8,128)(2,1)} fusion(bf16[32,16,2,1024]{3,2,1,0:T(2,128)(2,1)} %param.7, bf16[32,16]{1,0:T(8,128)(2,1)S(1)} %copy.8), kind=kLoop, calls=%fused_computation.1 | loop fusion | flops 1048576 | bytes 4195328 | tf_op jit(solution)/shard_map/transpose | solution.py:602
  5.4 126.8 %shard_map.73 = (s16[8,3,4,64,128]{4,3,2,1,0:T(8,128)(2,1)}, f32[8,16,128]{2,1,0:T(8,128)}, f32[16,128]{1,0:T(8,128)}, bf16[2,2,32,16,1024]{4,3,2,1,0:T(8,128)(2,1)}, bf16[2,2,32,16,1024]{4,3,2,1,0:T(8,128)(2,1)}) custom-call(s32[3]{0:T(128)} %plan.1, bf16[32,2,16,1024]{3,2,1,0:T(8,128)(2,1)} %fusion.m, bf16[16,128]{1,0:T(8,128)(2,1)} %pad.4.fl, ...), custom_call_target="tpu_custom_call" | custom-call | tf_op jit(solution)/shard_map/pallas_call | solution.py:476
  132.2 14.9 %shard_map.74 = f32[384,2048]{1,0:T(8,128)} custom-call(s16[8,12,2,32,128]{4,3,2,1,0:T(8,128)(2,1)} %bitcast.10, f32[8,16,128]{2,1,0:T(8,128)} %get-tuple-element.11.c_ref, f32[16,128]{1,0:T(8,128)} %get-tuple-element.12.inv_ref, bf16[2,1024,1024]{2,1,0:T(8,128)(2,1)} %bitcast.8, bf16[2,1024,1024]{2,1,0:T(8,128)(2,1)} %bitcast.9), custom_call_target="tpu_custom_call" | custom-call | tf_op jit(solution)/shard_map/pallas_call | solution.py:579
